TPU v7x, 32 devices: a whole 2x2x4 slice. The times are simulated.
32 devices in a mesh: expert: 4 (over y, x), zero: 8 (over z, core).
Axes of the slice: x: 2, y: 2, z: 4, core: 2. Of those that a mesh axis runs over, the one named last changes fastest.
Arguments:
- tokens: bfloat16 [4096, 1024], P(('expert', 'zero')), may hold values from -6 to 6
- grads_out: bfloat16 [4096, 1024], P(('expert', 'zero')), may hold values from -1.1953125 to 1.1953125
- routes: int32 [4096, 2], P(('expert', 'zero')), may hold values from 0 to 3, as said below
- slots: int32 [4096, 2], P(('expert', 'zero')), may hold values from 0 to 64, as said below
- combine: bfloat16 [4096, 2], P(('expert', 'zero')), may hold values from 0.049804688 to 1
- w_in: bfloat16 [4, 1024, 4096], P('expert', None, 'zero'), may hold values from -0.1875 to 0.1875
- b_in: bfloat16 [4, 4096], P('expert', 'zero'), may hold values from -3 to 3
- w_out: bfloat16 [4, 4096, 1024], P('expert', 'zero'), may hold values from -0.09375 to 0.09375
- b_out: bfloat16 [4, 1024], P('expert'), may hold values from -0.59765625 to 0.59765625
Outputs:
- grad_tokens: bfloat16 [4096, 1024], P(('expert', 'zero'))
- grad_combine: float32 [4096, 2], P(('expert', 'zero'))
- grad_w_in: bfloat16 [4, 1024, 4096], P('expert', None, 'zero')
- grad_b_in: float32 [4, 4096], P('expert', 'zero')
- grad_w_out: bfloat16 [4, 4096, 1024], P('expert', 'zero')
- grad_b_out: float32 [4, 1024], P('expert')
Inputs may be any that keep to these rules, and one draw needn't show every extreme that they name: `routes`: each row names 2 different experts. Within the rows of one device (aligned blocks of 128 rows), the choices that name one expert, taken in order of row and then of column, hold the slots 0, 1, 2 and so on; once 64 of them are taken, every further such choice holds 64 and is dropped.
All inputs are finite; a program needn't handle non-finite values.
Results may differ from a plain program's by a relative error of at most 0.0065.
Values may be sent and summed in bfloat16 or wider, within the bound.
A program may use at most 128 MiB of HBM per device.

v0:
```python
import jax
import jax.numpy as jnp
from jax import lax
from jax.sharding import PartitionSpec as P

TOP = 2


def gelu_parts(pre):
    cdf = 0.5 * (1.0 + lax.erf(pre * 0.7071067811865476))
    dens = jnp.exp(-0.5 * pre * pre) * 0.3989422804014327
    return (pre * cdf, cdf + pre * dens)


def forward_back(rows_x, rows_g, rows_c, weight_in, bias_in, weight_out):
    pre = (
        jnp.dot(rows_x, weight_in, preferred_element_type=jnp.float32)
        + bias_in.astype(jnp.float32)[None, :]
    )
    hidden32, slope = gelu_parts(pre)
    back = jnp.einsum("rd,fd->rf", rows_g, weight_out, preferred_element_type=jnp.float32)
    weight = rows_c.astype(jnp.float32)[:, None]
    inner = jnp.sum(hidden32 * back, axis=1)
    dout = (weight * rows_g.astype(jnp.float32)).astype(jnp.bfloat16)
    dpre = (weight * back * slope).astype(jnp.bfloat16)
    return (hidden32.astype(jnp.bfloat16), inner, dout, dpre)


def group_partials(left, right, groups):
    left_g = left.reshape(groups, -1, left.shape[1])
    right_g = right.reshape(groups, -1, right.shape[1])
    parts = jnp.einsum("nra,nrb->nab", left_g, right_g, preferred_element_type=jnp.float32).astype(
        jnp.bfloat16
    )
    parts = lax.optimization_barrier(parts)
    return jnp.sum(parts.astype(jnp.float32), axis=0).astype(jnp.bfloat16)


def on_device(tokens, grads_out, routes, slots, combine, w_in, b_in, w_out, b_out):
    n_expert = lax.axis_size("expert")
    n_zero = lax.axis_size("zero")
    tok_rows = tokens.shape[0]
    cap_rows = TOP * tok_rows // n_expert
    width = n_expert * cap_rows
    spots = jnp.arange(width, dtype=jnp.int32)
    places = jnp.where(slots < cap_rows, routes * cap_rows + slots, -1)
    picks = (places[:, :, None] == spots[None, None, :]).astype(jnp.bfloat16)
    both = picks[:, 0] + picks[:, 1]
    send_x = jnp.einsum("tp,td->pd", both, tokens, preferred_element_type=jnp.float32).astype(
        jnp.bfloat16
    )
    send_g = jnp.einsum("tp,td->pd", both, grads_out, preferred_element_type=jnp.float32).astype(
        jnp.bfloat16
    )
    send_c = jnp.einsum("tkp,tk->p", picks, combine, preferred_element_type=jnp.float32).astype(
        jnp.bfloat16
    )
    got_x, got_g, got_c = (
        lax.all_to_all(
            send_x.reshape(n_expert, cap_rows, -1),
            "expert",
            split_axis=0,
            concat_axis=0,
            tiled=True,
        ),
        lax.all_to_all(
            send_g.reshape(n_expert, cap_rows, -1),
            "expert",
            split_axis=0,
            concat_axis=0,
            tiled=True,
        ),
        lax.all_to_all(
            send_c.reshape(n_expert, cap_rows), "expert", split_axis=0, concat_axis=0, tiled=True
        ),
    )
    rows_x = got_x.reshape(width, -1)
    rows_g = got_g.reshape(width, -1)
    rows_c = got_c.reshape(width)
    bias_out = b_out[0].astype(jnp.float32)
    full_in, full_out, full_bias = (
        lax.all_gather(w_in, "zero", axis=2, tiled=True),
        lax.all_gather(w_out, "zero", axis=1, tiled=True),
        lax.all_gather(b_in, "zero", axis=1, tiled=True),
    )
    hidden, inner, dout, dpre = forward_back(
        rows_x, rows_g, rows_c, full_in[0], full_bias[0], full_out[0]
    )
    slot_dx = jnp.einsum("rf,df->rd", dpre, full_in[0], preferred_element_type=jnp.float32)
    slot_dc = inner + jnp.sum(rows_g.astype(jnp.float32) * bias_out[None, :], axis=1)
    all_hidden, all_dpre = (
        lax.all_to_all(hidden, "zero", split_axis=1, concat_axis=0, tiled=True),
        lax.all_to_all(dpre, "zero", split_axis=1, concat_axis=0, tiled=True),
    )
    all_x, all_dout = (
        lax.all_gather(rows_x, "zero", axis=0, tiled=True),
        lax.all_gather(dout, "zero", axis=0, tiled=True),
    )
    grad_w_in = group_partials(all_x, all_dpre, n_zero)[None]
    grad_w_out = group_partials(all_hidden, all_dout, n_zero)[None]
    grad_b_in = jnp.sum(all_dpre.astype(jnp.float32), axis=0)[None]
    grad_b_out = jnp.sum(all_dout.astype(jnp.float32), axis=0)[None]
    back_dx, back_dc = (
        lax.all_to_all(
            slot_dx.reshape(n_expert, cap_rows, -1),
            "expert",
            split_axis=0,
            concat_axis=0,
            tiled=True,
        ),
        lax.all_to_all(
            slot_dc.reshape(n_expert, cap_rows), "expert", split_axis=0, concat_axis=0, tiled=True
        ),
    )
    picks_wide = picks.astype(jnp.float32)
    grad_tokens = jnp.dot(
        picks_wide[:, 0] + picks_wide[:, 1],
        back_dx.reshape(width, -1),
        precision=lax.Precision.HIGHEST,
    ).astype(jnp.bfloat16)
    grad_combine = jnp.einsum(
        "tkp,p->tk", picks_wide, back_dc.reshape(width), precision=lax.Precision.HIGHEST
    )
    return (grad_tokens, grad_combine, grad_w_in, grad_b_in, grad_w_out, grad_b_out)


def solution(mesh):
    in_specs = (
        P(("expert", "zero"), None),
        P(("expert", "zero"), None),
        P(("expert", "zero"), None),
        P(("expert", "zero"), None),
        P(("expert", "zero"), None),
        P("expert", None, "zero"),
        P("expert", "zero"),
        P("expert", "zero", None),
        P("expert", None),
    )
    out_specs = (
        P(("expert", "zero"), None),
        P(("expert", "zero"), None),
        P("expert", None, "zero"),
        P("expert", "zero"),
        P("expert", "zero", None),
        P("expert", None),
    )
    return jax.shard_map(
        on_device, mesh=mesh, in_specs=in_specs, out_specs=out_specs, check_vma=False
    )
```

profile of v0, /device:TPU:0, one launch (start us, length us, event | category | flops | bytes accessed | tf_op | source)
XLA Modules:
  0.0 377.0 jit_solution(16114300347451899075)
XLA Ops:
  10.9 5.2 %all-to-all-start = ((bf16[4,1,64]{2,1,0:T(2,128)(2,1)}), bf16[4,1,64]{2,1,0:T(2,128)(2,1)S(1)}, u32[]{:S(2)}, u32[]{:S(2)}) async-start(bf16[4,1,64]{2,1,0:T(2,128)(2,1)} %all_to_all.55), calls=%async_computation | async-start | bytes 4096 | tf_op jit(solution)/shard_map/all_to_all | solution.py:73
  20.7 3.5 all-to-all-start.1
  24.3 6.8 %all-to-all-done.1 = bf16[4,64,1024]{2,1,0:T(8,128)(2,1)S(1)} async-done(((bf16[4,64,1024]{2,1,0:T(8,128)(2,1)}), bf16[4,64,1024]{2,1,0:T(8,128)(2,1)S(1)}, u32[]{:S(2)}, u32[]{:S(2)}) %all-to-all-start.1) | async-done | bytes 524320 | tf_op jit(solution)/shard_map/all_to_all | solution.py:66
  33.2 3.5 all-to-all-start.2
  36.7 14.2 %all_gather.17 = bf16[1,4096]{1,0:T(2,128)(2,1)S(1)} all-gather(bf16[1,512]{1,0:T(2,128)(2,1)S(1)} %copy-done.7), channel_id=1, replica_groups=mesh['expert'=4,'zero'=8] {'zero'}, dimensions={1}, use_global_device_ids=true | all-gather | bytes 9216 | tf_op jit(solution)/shard_map/all_gather | solution.py:84
  51.2 43.4 %all-gather.7.cloned.1.call-done = bf16[1,1024,4096]{2,1,0:T(8,128)(2,1)} async-done(((bf16[1,1024,512]{2,1,0:T(8,128)(2,1)}), bf16[1,1024,4096]{2,1,0:T(8,128)(2,1)}) %all-gather.7.cloned.1.call-update) | async-done | bytes 8388624 | tf_op jit(solution)/shard_map/all_gather | solution.py:82
  94.6 7.7 %fusion.6 = f32[256,4096]{1,0:T(8,128)} fusion(bf16[256,1024]{1,0:T(8,128)(2,1)S(1)} %bitcast.70, bf16[1,1024,4096]{2,1,0:T(8,128)(2,1)} %all-gather.7.cloned.1.call-done, f32[4096]{0:T(1024)S(1)} %bitcast.75), kind=kOutput, calls=%fused_computation.10 | convolution fusion | flops 2148532224 | bytes 13123584 | tf_op jit(solution)/shard_map/dot_general | solution.py:17
  102.3 74.5 %all-gather.5.cloned.1.call-done = bf16[1,4096,1024]{2,1,0:T(8,128)(2,1)} async-done(((bf16[1,512,1024]{2,1,0:T(8,128)(2,1)}), bf16[1,4096,1024]{2,1,0:T(8,128)(2,1)}) %all-gather.5.cloned.1.call-update) | async-done | bytes 8388624 | tf_op jit(solution)/shard_map/all_gather | solution.py:83
  176.7 8.0 %multiply_reduce_fusion = (f32[256]{0:T(256)S(1)}, bf16[256,4096]{1,0:T(8,128)(2,1)S(1)}, bf16[256,4096]{1,0:T(8,128)(2,1)}) fusion(f32[256,4096]{1,0:T(8,128)} %fusion.6, f32[256]{0:T(256)S(1)} %reshape.100, bf16[256,1024]{1,0:T(8,128)(2,1)S(1)} %bitcast.65, bf16[1,4096,1024]{2,1,0:T(8,128)(2,1)} %all-gather.5.cloned.1.call-done), kind=kOutput, calls=%fused_computation.18 | convolution fusion | flops 2163212032 | bytes 17303552 | tf_op jit(solution)/shard_map/rd,fd->rf/dot_general | solution.py:21
  185.6 3.7 all-to-all-start.4
  189.2 6.8 %fusion = f32[4,64,1024]{2,1,0:T(8,128)} fusion(bf16[4,64,4096]{2,1,0:T(8,128)(2,1)S(1)} %bitcast.68, bf16[1,1024,4096]{2,1,0:T(8,128)(2,1)} %all-gather.7.cloned.1.call-done), kind=kOutput, calls=%fused_computation | convolution fusion | flops 2147483648 | bytes 11534336 | tf_op jit(solution)/shard_map/rf,df->rd/dot_general | solution.py:89
  196.0 4.2 %all-to-all-start.3 = ((f32[4,64,1024]{2,1,0:T(8,128)}), f32[4,64,1024]{2,1,0:T(8,128)S(1)}, u32[]{:S(2)}, u32[]{:S(2)}) async-start(f32[4,64,1024]{2,1,0:T(8,128)} %fusion), calls=%async_computation.3 | async-start | bytes 2097152 | tf_op jit(solution)/shard_map/all_to_all | solution.py:104
  200.8 3.1 copy.33
  203.9 9.8 %all-to-all-done.3 = f32[4,64,1024]{2,1,0:T(8,128)S(1)} async-done(((f32[4,64,1024]{2,1,0:T(8,128)}), f32[4,64,1024]{2,1,0:T(8,128)S(1)}, u32[]{:S(2)}, u32[]{:S(2)}) %all-to-all-start.3) | async-done | bytes 1048608 | tf_op jit(solution)/shard_map/all_to_all | solution.py:104
  213.7 3.6 all-to-all-start.5
  217.3 4.1 %copy.28 = bf16[256,4096]{0,1:T(8,128)(2,1)} copy(bf16[256,4096]{1,0:T(8,128)(2,1)} %get-tuple-element.8) | data formatting | bytes 4194304 | tf_op jit(solution)/shard_map/all_to_all | solution.py:92
  221.5 73.6 %all-to-all-done.5 = bf16[256,8,512]{2,0,1:T(8,128)(2,1)S(1)} async-done(((bf16[256,8,512]{2,0,1:T(8,128)(2,1)}), bf16[256,8,512]{2,0,1:T(8,128)(2,1)S(1)}, u32[]{:S(2)}, u32[]{:S(2)}) %all-to-all-start.5) | async-done | bytes 2097184 | tf_op jit(solution)/shard_map/all_to_all | solution.py:93
  295.1 4.7 %all-to-all-start.6 = ((bf16[256,8,512]{0,2,1:T(8,128)(2,1)}), bf16[256,8,512]{0,2,1:T(8,128)(2,1)}, u32[]{:S(2)}, u32[]{:S(2)}) async-start(bf16[256,8,512]{0,2,1:T(8,128)(2,1)} %bitcast.63), calls=%async_computation.6 | async-start | bytes 4194304 | tf_op jit(solution)/shard_map/all_to_all | solution.py:92
  299.8 3.5 convert_reduce_fusion
  306.9 7.8 %convolution_convert_fusion.1 = bf16[8,1024,512]{2,1,0:T(8,128)(2,1)} fusion(bf16[8,256,1024]{2,1,0:T(8,128)(2,1)} %bitcast.66, bf16[256,8,512]{2,0,1:T(8,128)(2,1)S(1)} %all-to-all-done.5), kind=kOutput, calls=%fused_computation.8 | convolution fusion | flops 2151677952 | bytes 14680064 | tf_op jit(solution)/shard_map/nra,nrb->nab/dot_general | solution.py:32
  314.7 34.0 %all-to-all-done.6 = bf16[256,8,512]{0,2,1:T(8,128)(2,1)} async-done(((bf16[256,8,512]{0,2,1:T(8,128)(2,1)}), bf16[256,8,512]{0,2,1:T(8,128)(2,1)}, u32[]{:S(2)}, u32[]{:S(2)}) %all-to-all-start.6) | async-done | bytes 2097184 | tf_op jit(solution)/shard_map/all_to_all | solution.py:92
  348.6 8.4 %convolution_convert_fusion = bf16[8,512,1024]{2,1,0:T(8,128)(2,1)} fusion(bf16[8,256,1024]{2,1,0:T(8,128)(2,1)} %bitcast.62, bf16[256,8,512]{0,2,1:T(8,128)(2,1)} %all-to-all-done.6), kind=kOutput, calls=%fused_computation.7 | convolution fusion | flops 2151677952 | bytes 14680064 | tf_op jit(solution)/shard_map/nra,nrb->nab/dot_general | solution.py:32
  357.0 5.9 %reduce_sum.68 = bf16[1024,512]{1,0:T(8,128)(2,1)} reduce(bf16[8,1024,512]{2,1,0:T(8,128)(2,1)} %convolution_convert_fusion.1, bf16[]{:T(256)} %constant.18.clone.1), dimensions={0}, to_apply=%region_2.3 | reduce | flops 3670016 | bytes 9437186 | tf_op jit(solution)/shard_map/reduce_sum | solution.py:36
  362.9 6.7 %reduce_sum.70 = bf16[512,1024]{1,0:T(8,128)(2,1)} reduce(bf16[8,512,1024]{2,1,0:T(8,128)(2,1)} %convolution_convert_fusion, bf16[]{:T(256)} %constant.18.clone.1), dimensions={0}, to_apply=%region_4.5 | reduce | flops 3670016 | bytes 9437186 | tf_op jit(solution)/shard_map/reduce_sum | solution.py:36
  (50 shorter events, 16.6 us)
Async XLA Ops:
  7.2 9.8 %copy-start = (bf16[128,1024]{1,0:T(8,128)(2,1)S(1)}, bf16[128,1024]{1,0:T(8,128)(2,1)}, u32[]{:S(2)}) copy-start(bf16[128,1024]{1,0:T(8,128)(2,1)} %param.10) | copy-start | bytes 786436
  7.2 24.9 %copy-start.5 = (bf16[128,1024]{1,0:T(8,128)(2,1)S(1)}, bf16[128,1024]{1,0:T(8,128)(2,1)}, u32[]{:S(2)}) copy-start(bf16[128,1024]{1,0:T(8,128)(2,1)} %param.9) | copy-start | bytes 786436
  7.2 29.5 %copy-start.7 = (bf16[1,512]{1,0:T(2,128)(2,1)S(1)}, bf16[1,512]{1,0:T(2,128)(2,1)}, u32[]{:S(2)}) copy-start(bf16[1,512]{1,0:T(2,128)(2,1)} %param.15) | copy-start | bytes 3076
  7.2 43.7 %copy-start.6 = (bf16[1,1024]{1,0:T(2,128)(2,1)S(1)}, bf16[1,1024]{1,0:T(2,128)(2,1)}, u32[]{:S(2)}) copy-start(bf16[1,1024]{1,0:T(2,128)(2,1)} %param.17) | copy-start | bytes 6148
  7.2 87.4 %all-gather.7.cloned.1.call-start = ((), (), s32[]{:S(2)}) async-start(), calls=%async_computation.8 | async-start | bytes 9437184 | tf_op jit(solution)/shard_map/all_gather | solution.py:82
  7.9 168.8 %all-gather.5.cloned.1.call-start = ((), (), s32[]{:S(2)}) async-start(), calls=%async_computation.7 | async-start | bytes 9437184 | tf_op jit(solution)/shard_map/all_gather | solution.py:83
  10.9 9.7 %all-to-all-start = ((bf16[4,1,64]{2,1,0:T(2,128)(2,1)}), bf16[4,1,64]{2,1,0:T(2,128)(2,1)S(1)}, u32[]{:S(2)}, u32[]{:S(2)}) async-start(bf16[4,1,64]{2,1,0:T(2,128)(2,1)} %all_to_all.55), calls=%async_computation | async-start | bytes 4096 | tf_op jit(solution)/shard_map/all_to_all | solution.py:73
  20.7 10.4 %all-to-all-start.1 = ((bf16[4,64,1024]{2,1,0:T(8,128)(2,1)}), bf16[4,64,1024]{2,1,0:T(8,128)(2,1)S(1)}, u32[]{:S(2)}, u32[]{:S(2)}) async-start(bf16[4,64,1024]{2,1,0:T(8,128)(2,1)} %bitcast.4), calls=%async_computation.1 | async-start | bytes 1048576 | tf_op jit(solution)/shard_map/all_to_all | solution.py:66
  24.2 275.6 %all-gather.11.cloned.1.call-start = ((), (), s32[]{:S(2)}) async-start(), calls=%async_computation.10 | async-start | bytes 4718592 | tf_op jit(solution)/shard_map/all_gather | solution.py:97
  33.2 18.0 %all-to-all-start.2 = ((bf16[4,64,1024]{2,1,0:T(8,128)(2,1)}), bf16[4,64,1024]{2,1,0:T(8,128)(2,1)S(1)}, u32[]{:S(2)}, u32[]{:S(2)}) async-start(bf16[4,64,1024]{2,1,0:T(8,128)(2,1)} %bitcast.7), calls=%async_computation.2 | async-start | bytes 1048576 | tf_op jit(solution)/shard_map/all_to_all | solution.py:59
  51.2 51.1 %copy-start.3 = (bf16[4,64,1024]{2,1,0:T(8,128)(2,1)}, bf16[4,64,1024]{2,1,0:T(8,128)(2,1)S(1)}, u32[]{:S(2)}) copy-start(bf16[4,64,1024]{2,1,0:T(8,128)(2,1)S(1)} %all-to-all-done.2) | copy-start | bytes 1572868
  184.8 11.2 %copy-start.2 = (bf16[256,4096]{1,0:T(8,128)(2,1)}, bf16[256,4096]{1,0:T(8,128)(2,1)S(1)}, u32[]{:S(2)}) copy-start(bf16[256,4096]{1,0:T(8,128)(2,1)S(1)} %get-tuple-element.7) | copy-start | bytes 6291460
  185.6 10.4 %all-to-all-start.4 = ((f32[4,1,64]{2,1,0:T(1,128)}), f32[4,1,64]{2,1,0:T(1,128)S(1)}, u32[]{:S(2)}, u32[]{:S(2)}) async-start(f32[4,1,64]{2,1,0:T(1,128)} %add.60), calls=%async_computation.4 | async-start | bytes 4096 | tf_op jit(solution)/shard_map/all_to_all | solution.py:111
  196.0 17.7 %all-to-all-start.3 = ((f32[4,64,1024]{2,1,0:T(8,128)}), f32[4,64,1024]{2,1,0:T(8,128)S(1)}, u32[]{:S(2)}, u32[]{:S(2)}) async-start(f32[4,64,1024]{2,1,0:T(8,128)} %fusion), calls=%async_computation.3 | async-start | bytes 2097152 | tf_op jit(solution)/shard_map/all_to_all | solution.py:104
  200.2 106.6 %all-gather.9.cloned.1.call-start = ((), (), s32[]{:S(2)}) async-start(), calls=%async_computation.9 | async-start | bytes 4718592 | tf_op jit(solution)/shard_map/all_gather | solution.py:96
  213.7 81.4 %all-to-all-start.5 = ((bf16[256,8,512]{2,0,1:T(8,128)(2,1)}), bf16[256,8,512]{2,0,1:T(8,128)(2,1)S(1)}, u32[]{:S(2)}, u32[]{:S(2)}) async-start(bf16[256,8,512]{2,0,1:T(8,128)(2,1)} %bitcast.64), calls=%async_computation.5 | async-start | bytes 4194304 | tf_op jit(solution)/shard_map/all_to_all | solution.py:93
  295.1 10.4 %copy-start.4 = (f32[128,2,256]{2,0,1:T(8,128)S(1)}, f32[128,2,256]{2,0,1:T(8,128)}, u32[]{:S(2)}) copy-start(f32[128,2,256]{2,0,1:T(8,128)} %get-tuple-element.9) | copy-start | bytes 786436
  295.1 53.5 %all-to-all-start.6 = ((bf16[256,8,512]{0,2,1:T(8,128)(2,1)}), bf16[256,8,512]{0,2,1:T(8,128)(2,1)}, u32[]{:S(2)}, u32[]{:S(2)}) async-start(bf16[256,8,512]{0,2,1:T(8,128)(2,1)} %bitcast.63), calls=%async_computation.6 | async-start | bytes 4194304 | tf_op jit(solution)/shard_map/all_to_all | solution.py:92
  357.0 13.4 %copy-start.1 = (bf16[128,1024]{1,0:T(8,128)(2,1)S(1)}, bf16[128,1024]{1,0:T(8,128)(2,1)}, u32[]{:S(2)}) copy-start(bf16[128,1024]{1,0:T(8,128)(2,1)} %param.10) | copy-start | bytes 786436
Sparse Core Ops, SparseCore 0:
  9.7 84.8 all-gather.6
  96.2 80.5 all-gather.4
  178.4 47.3 all-gather.10
  227.8 74.9 all-gather.8
where the time goes:
time: 378 us; the launch traced here: 377 us
  waiting for transfers between devices  247 us (65%)
  matrix products  44.1 us (12%)
  starting transfers between devices  28.4 us (8%)
  other arithmetic  21 us (6%)
  blocking collectives  14.2 us (4%)
  between operations  13.9 us (4%)
  local copies, waits for them, and re-layouts  8.74 us (2%)
    all_gather x1, waiting for transfers between devices, on_device(): lax.all_gather(w_out, 'zero', axis=1, tiled=True)  74.5 us
    all_to_all x1, waiting for transfers between devices, on_device(): lax.all_to_all(dpre, 'zero', split_axis=1, concat_axis=0, tiled=True)  73.6 us
    all_gather x1, waiting for transfers between devices, on_device(): lax.all_gather(w_in, 'zero', axis=2, tiled=True)  43.4 us
    all_to_all x1, waiting for transfers between devices, on_device(): lax.all_to_all(hidden, 'zero', split_axis=1, concat_axis=0, tiled=True)  34 us
    dot_general x2, matrix products, group_partials(): jnp.einsum('nra,nrb->nab', left_g, right_g, preferred_element_type=jnp.fl...  16.2 us
    all_gather x1, blocking collectives, on_device(): lax.all_gather(b_in, 'zero', axis=1, tiled=True)  14.2 us
    reduce_sum x2, other arithmetic, group_partials(): return jnp.sum(parts.astype(jnp.float32), axis=0).astype(jnp.bfloat16)  12.5 us
    all_to_all x1, waiting for transfers between devices, on_device(): lax.all_to_all(slot_dx.reshape(n_expert, cap_rows, -1), 'expert', split_a...  9.79 us
  transfers between devices with their start and end apart: 11, of which 7 were waited for; matrix products, arithmetic and copies ran while one was open for 14% of the time, Pallas kernels for 0%

commit v1 on v0

v1 whole, which is shorter than its diff:
```python
import jax
import jax.numpy as jnp
from jax import lax
from jax.sharding import PartitionSpec as P

TOP = 2


def gelu_parts(pre):
    cdf = 0.5 * (1.0 + lax.erf(pre * 0.7071067811865476))
    dens = jnp.exp(-0.5 * pre * pre) * 0.3989422804014327
    return (pre * cdf, cdf + pre * dens)


def on_device(tokens, grads_out, routes, slots, combine, w_in, b_in, w_out, b_out):
    f32, bf16 = jnp.float32, jnp.bfloat16
    n_expert = lax.axis_size("expert")
    n_zero = lax.axis_size("zero")
    tok_rows, dim = tokens.shape
    cap_rows = TOP * tok_rows // n_expert
    width = n_expert * cap_rows
    spots = jnp.arange(width, dtype=jnp.int32)
    places = jnp.where(slots < cap_rows, routes * cap_rows + slots, -1)
    picks = (places[:, :, None] == spots[None, None, :]).astype(bf16)
    both = picks[:, 0] + picks[:, 1]
    pair = jnp.concatenate([tokens, grads_out], axis=1)
    send = jnp.einsum("tp,td->pd", both, pair, preferred_element_type=f32).astype(bf16)
    send_c = jnp.einsum("tkp,tk->p", picks, combine, preferred_element_type=f32).astype(bf16)
    send = jnp.concatenate([send, jnp.broadcast_to(send_c[:, None], (width, 128))], axis=1)
    got = lax.all_to_all(
        send.reshape(n_expert, cap_rows, -1), "expert", split_axis=0, concat_axis=0, tiled=True
    ).reshape(width, -1)
    rows = lax.all_gather(got, "zero", axis=0, tiled=True)
    rows_x = rows[:, :dim]
    rows_g = rows[:, dim : 2 * dim]
    weight = rows[:, 2 * dim : 2 * dim + 1].astype(f32)
    pre = jnp.dot(rows_x, w_in[0], preferred_element_type=f32) + b_in.astype(f32)
    hidden32, slope = gelu_parts(pre)
    back = jnp.einsum("rd,fd->rf", rows_g, w_out[0], preferred_element_type=f32)
    inner = jnp.sum(hidden32 * back, axis=1)
    hidden = hidden32.astype(bf16)
    dpre = (weight * back * slope).astype(bf16)
    dout = (weight * rows_g.astype(f32)).astype(bf16)
    slot_dx = jnp.einsum("rf,df->rd", dpre, w_in[0], preferred_element_type=f32).astype(bf16)
    part_dx = lax.all_to_all(
        slot_dx.reshape(n_zero, width, dim), "zero", split_axis=0, concat_axis=0, tiled=True
    )
    sum_dx = jnp.sum(part_dx.astype(f32), axis=0).astype(bf16)
    part_dc = lax.all_to_all(
        inner.reshape(n_zero, width), "zero", split_axis=0, concat_axis=0, tiled=True
    )
    bias_dc = jnp.sum(got[:, dim : 2 * dim].astype(f32) * b_out.astype(f32), axis=1)
    sum_dc = jnp.sum(part_dc, axis=0) + bias_dc
    grad_w_in = jnp.einsum("ra,rb->ab", rows_x, dpre, preferred_element_type=f32).astype(bf16)
    grad_w_out = jnp.einsum("ra,rb->ab", hidden, dout, preferred_element_type=f32).astype(bf16)
    grad_b_in = jnp.sum(dpre.astype(f32), axis=0)
    grad_b_out = jnp.sum(dout.astype(f32), axis=0)
    back_dx, back_dc = (
        lax.all_to_all(
            sum_dx.reshape(n_expert, cap_rows, -1), "expert", split_axis=0, concat_axis=0, tiled=True
        ),
        lax.all_to_all(
            sum_dc.reshape(n_expert, cap_rows), "expert", split_axis=0, concat_axis=0, tiled=True
        ),
    )
    grad_tokens = jnp.dot(
        both, back_dx.reshape(width, -1), preferred_element_type=f32
    ).astype(bf16)
    grad_combine = jnp.sum(picks.astype(f32) * back_dc.reshape(width), axis=2)
    return (grad_tokens, grad_combine, grad_w_in[None], grad_b_in[None], grad_w_out[None], grad_b_out[None])


def solution(mesh):
    in_specs = (
        P(("expert", "zero"), None),
        P(("expert", "zero"), None),
        P(("expert", "zero"), None),
        P(("expert", "zero"), None),
        P(("expert", "zero"), None),
        P("expert", None, "zero"),
        P("expert", "zero"),
        P("expert", "zero", None),
        P("expert", None),
    )
    out_specs = (
        P(("expert", "zero"), None),
        P(("expert", "zero"), None),
        P("expert", None, "zero"),
        P("expert", "zero"),
        P("expert", "zero", None),
        P("expert", None),
    )
    return jax.shard_map(
        on_device, mesh=mesh, in_specs=in_specs, out_specs=out_specs, check_vma=False
    )
```

time: 378 us -> 272 us (0.72)
  waiting for transfers between devices: 247 us -> 173 us
  starting transfers between devices: 28.4 us -> 16.4 us
  matrix products: 44.1 us -> 34.1 us
  other arithmetic: 21 us -> 12.5 us
  local copies, waits for them, and re-layouts: 8.74 us -> 1.39 us
  blocking collectives: 14.2 us -> 20.1 us
    all_to_all x7 -> x4, waiting for transfers between devices: 127 us -> 87 us  [the longest x1 85.1 us: on_device(): lax.all_to_all(slot_dx.reshape(n_zero, width, dim), 'zero', split_axis=0,...]
    all_gather x4 -> x1, waiting for transfers between devices: 118 us -> 86.1 us  [on_device(): rows = lax.all_gather(got, 'zero', axis=0, tiled=True)]
    all_to_all x0 -> x1, blocking collectives: none -> 20.1 us  [on_device(): lax.all_to_all(send.reshape(n_expert, cap_rows, -1), 'expert', split_axis...]
    all_gather x1 -> x0, blocking collectives: 14.2 us -> none  [on_device(): lax.all_gather(b_in, 'zero', axis=1, tiled=True)]
    all_to_all x7 -> x4, starting transfers between devices: 28.3 us -> 16.4 us  [the longest x1 5.16 us: on_device(): lax.all_to_all(slot_dx.reshape(n_zero, width, dim), 'zero', split_axis=0,...]
    dot_general x10 -> x8, matrix products: 44.1 us -> 34.1 us  [the longest x1 7.1 us: on_device(): jnp.einsum('ra,rb->ab', hidden, dout, preferred_element_type=f32)]
    all_to_all x4 -> x1, local copies, waits for them, and re-layouts: 8.45 us -> 0.51 us  [on_device(): lax.all_to_all(sum_dc.reshape(n_expert, cap_rows), 'expert', split_axis=0...]
    reduce_sum x5, other arithmetic: 17.1 us -> 9.36 us  [the longest x1 4.05 us: on_device(): sum_dx = jnp.sum(part_dx.astype(f32), axis=0).astype(bf16)]
  transfers between devices with their start and end apart: 11 -> 5, of which waited for: 7 -> 3; matrix products, arithmetic and copies ran while one was open for 14% -> 11% of each run, Pallas kernels for 0% -> 0%
where the time goes in v1:
time: 272 us
  waiting for transfers between devices  173 us (64%)
  matrix products  34.1 us (13%)
  blocking collectives  20.1 us (7%)
  starting transfers between devices  16.4 us (6%)
  between operations  14.2 us (5%)
  other arithmetic  12.5 us (5%)
    all_gather x1, waiting for transfers between devices, on_device(): rows = lax.all_gather(got, 'zero', axis=0, tiled=True)  86.1 us
    all_to_all x1, waiting for transfers between devices, on_device(): lax.all_to_all(slot_dx.reshape(n_zero, width, dim), 'zero', split_axis=0,...  85.1 us
    all_to_all x1, blocking collectives, on_device(): lax.all_to_all(send.reshape(n_expert, cap_rows, -1), 'expert', split_axis...  20.1 us
    dot_general x1, matrix products, on_device(): jnp.einsum('ra,rb->ab', hidden, dout, preferred_element_type=f32)  7.1 us
    dot_general x1, matrix products, on_device(): jnp.dot(rows_x, w_in[0], preferred_element_type=f32) + b_in.astype(f32)  6.86 us
    dot_general x1, matrix products, on_device(): jnp.einsum('ra,rb->ab', rows_x, dpre, preferred_element_type=f32)  6.21 us
    dot_general x1, matrix products, on_device(): jnp.einsum('rf,df->rd', dpre, w_in[0], preferred_element_type=f32)  5.93 us
  transfers between devices with their start and end apart: 5, of which 3 were waited for; matrix products, arithmetic and copies ran while one was open for 11% of the time, Pallas kernels for 0%

profile of v1, /device:TPU:0, one launch (start us, length us, event | category | flops | bytes accessed | tf_op | source)
XLA Modules:
  0.0 271.8 jit_solution(735948451423484692)
XLA Ops:
  7.2 0.8 compare_select_fusion
  8.2 0.9 fusion.32
  9.1 1.5 convolution_convert_fusion.1
  10.8 20.1 %all_to_all.30 = bf16[4,64,2176]{2,1,0:T(8,128)(2,1)} all-to-all(bf16[4,64,2176]{2,1,0:T(8,128)(2,1)S(1)} %bitcast.35), channel_id=1, replica_groups=mesh['expert'=4,'zero'=8] {'expert'}, dimensions={0} | all-to-all | bytes 2228224 | tf_op jit(solution)/shard_map/all_to_all | solution.py:30
  30.9 86.1 %all-gather.2.cloned.1.call-done = bf16[2048,2176]{1,0:T(8,128)(2,1)} async-done(((bf16[256,2176]{1,0:T(8,128)(2,1)}), bf16[2048,2176]{1,0:T(8,128)(2,1)}) %all-gather.2.cloned.1.call-update) | async-done | bytes 8912912 | tf_op jit(solution)/shard_map/all_gather | solution.py:33
  117.0 1.4 convert_reduce_fusion.2
  118.4 4.7 %fusion.10 = f32[2048,512]{1,0:T(8,128)S(1)} fusion(bf16[2048,2176]{1,0:T(8,128)(2,1)} %all-gather.2.cloned.1.call-done, bf16[1,512,1024]{2,1,0:T(8,128)(2,1)S(1)} %copy-done.3), kind=kOutput, calls=%fused_computation.17 | convolution fusion | flops 2147483648 | bytes 9437184 | tf_op jit(solution)/shard_map/rd,fd->rf/dot_general | solution.py:39
  123.2 6.9 %convert_reduce_fusion.1 = (f32[512]{0:T(512)}, bf16[2048,512]{1,0:T(8,128)(2,1)}, f32[2048]{0:T(1024)}, f32[2048,512]{1,0:T(8,128)}) fusion(f32[512]{0:T(512)S(1)} %bitcast.42, f32[2048,512]{1,0:T(8,128)S(1)} %fusion.10, f32[2048]{0:T(1024)S(1)} %convert_reduce_fusion.2, bf16[1,1024,512]{2,1,0:T(8,128)(2,1)S(1)} %copy-done, bf16[2048,2176]{1,0:T(8,128)(2,1)S(1)} %bitcast.38), kind=kOutput, calls=%fused_computation.9 | convolution fusion | flops 2165306880 | bytes 15749120 | tf_op jit(solution)/shard_map/dot_general | solution.py:37
  130.1 3.3 %all-to-all-start.3 = ((f32[8,1,256]{2,1,0:T(1,128)}), f32[8,1,256]{2,1,0:T(1,128)S(1)}, u32[]{:S(2)}, u32[]{:S(2)}) async-start(f32[8,1,256]{2,1,0:T(1,128)} %bitcast.11), calls=%async_computation.3 | async-start | bytes 16384 | tf_op jit(solution)/shard_map/all_to_all | solution.py:49
  133.4 5.9 %convolution_convert_fusion = bf16[2048,1024]{1,0:T(8,128)(2,1)} fusion(bf16[2048,512]{1,0:T(8,128)(2,1)} %get-tuple-element.7, bf16[1,1024,512]{2,1,0:T(8,128)(2,1)S(1)} %copy-done), kind=kOutput, calls=%fused_computation.12 | convolution fusion | flops 2149580800 | bytes 7340032 | tf_op jit(solution)/shard_map/rf,df->rd/dot_general | solution.py:44
  139.4 5.2 %all-to-all-start.1 = ((bf16[8,256,1024]{2,1,0:T(8,128)(2,1)}), bf16[8,256,1024]{2,1,0:T(8,128)(2,1)}, u32[]{:S(2)}, u32[]{:S(2)}) async-start(bf16[8,256,1024]{2,1,0:T(8,128)(2,1)} %bitcast.36), calls=%async_computation.1 | async-start | bytes 8388608 | tf_op jit(solution)/shard_map/all_to_all | solution.py:45
  144.5 1.2 multiply_reduce_fusion.1
  145.8 7.1 %fusion.23 = bf16[1,512,1024]{2,1,0:T(8,128)(2,1)} fusion(f32[2048,512]{1,0:T(8,128)} %get-tuple-element.9, f32[512]{0:T(512)S(1)} %bitcast.43, f32[2048]{0:T(1024)S(1)} %convert_reduce_fusion.2, bf16[2048,2176]{1,0:T(8,128)(2,1)} %all-gather.2.cloned.1.call-done), kind=kOutput, calls=%fused_computation.26 | convolution fusion | flops 2160590848 | bytes 9447424 | tf_op jit(solution)/shard_map/ra,rb->ab/dot_general | solution.py:55
  152.9 0.7 add.57
  153.6 85.1 %all-to-all-done.1 = bf16[8,256,1024]{2,1,0:T(8,128)(2,1)} async-done(((bf16[8,256,1024]{2,1,0:T(8,128)(2,1)}), bf16[8,256,1024]{2,1,0:T(8,128)(2,1)}, u32[]{:S(2)}, u32[]{:S(2)}) %all-to-all-start.1) | async-done | bytes 4194336 | tf_op jit(solution)/shard_map/all_to_all | solution.py:45
  238.6 3.7 %all-to-all-start.4 = ((f32[4,1,64]{2,1,0:T(1,128)}), f32[4,1,64]{2,1,0:T(1,128)S(1)}, u32[]{:S(2)}, u32[]{:S(2)}) async-start(f32[4,1,64]{2,1,0:T(1,128)} %add.57), calls=%async_computation.4 | async-start | bytes 4096 | tf_op jit(solution)/shard_map/all_to_all | solution.py:62
  242.3 6.2 %fusion.20 = bf16[1,1024,512]{2,1,0:T(8,128)(2,1)} fusion(bf16[2048,512]{1,0:T(8,128)(2,1)} %get-tuple-element.7, bf16[2048,2176]{1,0:T(8,128)(2,1)} %all-gather.2.cloned.1.call-done), kind=kOutput, calls=%fused_computation.25 | convolution fusion | flops 2148007936 | bytes 7340032 | tf_op jit(solution)/shard_map/ra,rb->ab/dot_general | solution.py:54
  248.5 4.1 %reduce_sum.66 = bf16[256,1024]{1,0:T(8,128)(2,1)} reduce(bf16[8,256,1024]{2,1,0:T(8,128)(2,1)} %all-to-all-done.1, bf16[]{:T(256)} %constant.16.clone.1), dimensions={0}, to_apply=%region_0.1 | reduce | flops 1835008 | bytes 4718594 | tf_op jit(solution)/shard_map/reduce_sum | solution.py:48
  252.6 4.2 %all-to-all-start.2 = ((bf16[4,64,1024]{2,1,0:T(8,128)(2,1)}), bf16[4,64,1024]{2,1,0:T(8,128)(2,1)S(1)}, u32[]{:S(2)}, u32[]{:S(2)}) async-start(bf16[4,64,1024]{2,1,0:T(8,128)(2,1)} %bitcast.9), calls=%async_computation.2 | async-start | bytes 1048576 | tf_op jit(solution)/shard_map/all_to_all | solution.py:59
  256.8 3.3 %convert_reduce_fusion = f32[1024]{0:T(1024)} fusion(bf16[2048,2176]{1,0:T(8,128)(2,1)} %all-gather.2.cloned.1.call-done, f32[2048]{0:T(1024)S(1)} %convert_reduce_fusion.2), kind=kLoop, calls=%fused_computation | loop fusion | flops 10484736 | bytes 4206592 | tf_op jit(solution)/shard_map/reduce_sum | solution.py:57
  260.6 0.7 reduce.7
  261.3 0.8 multiply_reduce_fusion.2
  262.1 1.9 all-to-all-done.2
  264.0 0.9 convolution_convert_fusion.2
  (29 shorter events, 1.0 us)
Async XLA Ops:
  7.2 116.0 %copy-start = (bf16[1,1024,512]{2,1,0:T(8,128)(2,1)S(1)}, bf16[1,1024,512]{2,1,0:T(8,128)(2,1)}, u32[]{:S(2)}) copy-start(bf16[1,1024,512]{2,1,0:T(8,128)(2,1)} %param.14) | copy-start | bytes 3145732
  7.2 23.7 %copy-start.2 = (bf16[1,512]{1,0:T(2,128)(2,1)S(1)}, bf16[1,512]{1,0:T(2,128)(2,1)}, u32[]{:S(2)}) copy-start(bf16[1,512]{1,0:T(2,128)(2,1)} %param.15) | copy-start | bytes 3076
  7.2 111.2 %copy-start.3 = (bf16[1,512,1024]{2,1,0:T(8,128)(2,1)S(1)}, bf16[1,512,1024]{2,1,0:T(8,128)(2,1)}, u32[]{:S(2)}) copy-start(bf16[1,512,1024]{2,1,0:T(8,128)(2,1)} %param.16) | copy-start | bytes 3145732
  7.2 109.8 %all-gather.2.cloned.1.call-start = ((), (), s32[]{:S(2)}) async-start(), calls=%async_computation.5 | async-start | bytes 10027008 | tf_op jit(solution)/shard_map/all_gather | solution.py:33
  117.0 6.2 %slice-start = ((s8[8912896]{0:T(1024)(128)(4,1)}), s8[4194304]{0:T(1024)(128)(4,1)S(1)}, s32[]{:S(2)}) async-start(s8[8912896]{0:T(1024)(128)(4,1)} %bitcast.37), calls=%async_computation.6 | async-start | bytes 8388608
  118.4 4.8 %slice-start.1 = ((s8[8912896]{0:T(1024)(128)(4,1)}), s8[4194304]{0:T(1024)(128)(4,1)S(1)}, s32[]{:S(2)}) async-start(s8[8912896]{0:T(1024)(128)(4,1)} %bitcast.37), calls=%async_computation.7 | async-start | bytes 8388608
  118.4 4.8 %slice-start.2 = ((s8[8912896]{0:T(1024)(128)(4,1)}), s8[524288]{0:T(1024)(128)(4,1)S(1)}, s32[]{:S(2)}) async-start(s8[8912896]{0:T(1024)(128)(4,1)} %bitcast.37), calls=%async_computation.8 | async-start | bytes 1048576
  130.1 9.3 %all-to-all-start.3 = ((f32[8,1,256]{2,1,0:T(1,128)}), f32[8,1,256]{2,1,0:T(1,128)S(1)}, u32[]{:S(2)}, u32[]{:S(2)}) async-start(f32[8,1,256]{2,1,0:T(1,128)} %bitcast.11), calls=%async_computation.3 | async-start | bytes 16384 | tf_op jit(solution)/shard_map/all_to_all | solution.py:49
  139.3 5.2 %copy-start.1 = (bf16[1,1024]{1,0:T(2,128)(2,1)S(1)}, bf16[1,1024]{1,0:T(2,128)(2,1)}, u32[]{:S(2)}) copy-start(bf16[1,1024]{1,0:T(2,128)(2,1)} %param.17) | copy-start | bytes 6148
  139.4 99.3 %all-to-all-start.1 = ((bf16[8,256,1024]{2,1,0:T(8,128)(2,1)}), bf16[8,256,1024]{2,1,0:T(8,128)(2,1)}, u32[]{:S(2)}, u32[]{:S(2)}) async-start(bf16[8,256,1024]{2,1,0:T(8,128)(2,1)} %bitcast.36), calls=%async_computation.1 | async-start | bytes 8388608 | tf_op jit(solution)/shard_map/all_to_all | solution.py:45
  238.6 14.0 %all-to-all-start.4 = ((f32[4,1,64]{2,1,0:T(1,128)}), f32[4,1,64]{2,1,0:T(1,128)S(1)}, u32[]{:S(2)}, u32[]{:S(2)}) async-start(f32[4,1,64]{2,1,0:T(1,128)} %add.57), calls=%async_computation.4 | async-start | bytes 4096 | tf_op jit(solution)/shard_map/all_to_all | solution.py:62
  252.6 11.5 %all-to-all-start.2 = ((bf16[4,64,1024]{2,1,0:T(8,128)(2,1)}), bf16[4,64,1024]{2,1,0:T(8,128)(2,1)S(1)}, u32[]{:S(2)}, u32[]{:S(2)}) async-start(bf16[4,64,1024]{2,1,0:T(8,128)(2,1)} %bitcast.9), calls=%async_computation.2 | async-start | bytes 1048576 | tf_op jit(solution)/shard_map/all_to_all | solution.py:59
Sparse Core Ops, SparseCore 0:
  31.0 85.9 all-gather.1

commit v2 on v1

--- a/solution.py
+++ b/solution.py
@@ -1,6 +1,10 @@
+import functools
+
 import jax
 import jax.numpy as jnp
 from jax import lax
+from jax.experimental import pallas as pl
+from jax.experimental.pallas import tpu as pltpu
 from jax.sharding import PartitionSpec as P
 
 TOP = 2
@@ -12,7 +16,7 @@
     return (pre * cdf, cdf + pre * dens)
 
 
-def on_device(tokens, grads_out, routes, slots, combine, w_in, b_in, w_out, b_out):
+def plain_device(tokens, grads_out, routes, slots, combine, w_in, b_in, w_out, b_out):
     f32, bf16 = jnp.float32, jnp.bfloat16
     n_expert = lax.axis_size("expert")
     n_zero = lax.axis_size("zero")
@@ -70,6 +74,348 @@
     return (grad_tokens, grad_combine, grad_w_in[None], grad_b_in[None], grad_w_out[None], grad_b_out[None])
 
 
+F32, BF16 = jnp.float32, jnp.bfloat16
+CORES = 2
+LANES = 128
+
+
+def matmul(left, right, dims):
+    return lax.dot_general(left, right, (dims, ((), ())), preferred_element_type=F32)
+
+
+def split_pair(value, rows):
+    high = value.astype(BF16).astype(F32)
+    lane = lax.broadcasted_iota(jnp.int32, (rows, LANES), 1)
+    return jnp.where(lane < LANES // 2, high, value - high).astype(BF16)
+
+
+def join_pair(pair):
+    return jnp.sum(pair.astype(F32), axis=1, keepdims=True) * (2.0 / LANES)
+
+
+def fused_kernel(
+    n_expert, chips, cap, pay_ref, w_in_ref, b_in_ref, w_out_ref, b_out_ref,
+    gt_ref, gc_ref, gwi_ref, gbi_ref, gwo_ref, gbo_ref,
+    tok, sendbuf, rows, hid, dpre, dout, dx, dxrecv, retsend, retrecv, fsend, frecv, facc,
+    tok_s, tok_r, xy_s, xy_r, sib_s, sib_r, dx_s, dx_r, ret_s, ret_r, fin_s, fin_r,
+):
+    me_e = lax.axis_index("expert")
+    me_z = lax.axis_index("zero")
+    chip, core = me_z // CORES, me_z % CORES
+    width = n_expert * cap
+    toks = tok.shape[1]
+    dim = w_in_ref.shape[0]
+    units = w_in_ref.shape[1]
+    sibling = (me_e, chip * CORES + 1 - core)
+
+    def chunk(index):
+        return pl.ds(pl.multiple_of(index * cap, cap), cap)
+
+    def expert_peer(p):
+        return lax.rem(me_e + p, n_expert)
+
+    def chip_peer(p):
+        return lax.rem(chip + p, chips)
+
+    def order(step):
+        low = chip
+        high = chips - 1 - chip
+        least = jnp.minimum(low, high)
+        half = (step + 1) // 2
+        near = jnp.where(step % 2 == 1, chip + half, chip - half)
+        far = jnp.where(low < high, step, chips - 1 - step)
+        return jnp.where(step <= 2 * least, near, far)
+
+    def remote(src, dst, send, recv, device):
+        return pltpu.make_async_remote_copy(
+            src_ref=src, dst_ref=dst, send_sem=send, recv_sem=recv, device_id=device,
+            device_id_type=pl.DeviceIdType.MESH,
+        )
+
+    def tok_copy(to, frm):
+        return remote(
+            tok.at[frm], tok.at[frm], tok_s.at[to], tok_r.at[frm], (me_e, to * CORES + core)
+        )
+
+    def xy_copy(src, peer, frm):
+        return remote(
+            sendbuf.at[src, chunk(peer)], rows.at[src * CORES + core, chunk(frm)],
+            xy_s.at[src, peer], xy_r.at[src, frm], (peer, me_z),
+        )
+
+    def sib_copy(src, e, lane):
+        return remote(
+            rows.at[src * CORES + lane, chunk(e)], rows.at[src * CORES + lane, chunk(e)],
+            sib_s.at[src, e], sib_r.at[src, e], sibling,
+        )
+
+    def dx_copy(src, lane):
+        return remote(
+            dx.at[src * CORES + lane], dxrecv.at[src], dx_s.at[src], dx_r.at[src], sibling
+        )
+
+    def ret_copy(src, peer, frm):
+        return remote(
+            retsend.at[src, chunk(peer)], retrecv.at[src, chunk(frm)],
+            ret_s.at[src, peer], ret_r.at[src, frm], (peer, me_z),
+        )
+
+    def fin_copy(to, frm):
+        return remote(
+            fsend.at[to], frecv.at[frm], fin_s.at[to], fin_r.at[frm], (me_e, to * CORES + core)
+        )
+
+    def picks_of(src):
+        meta = tok[src, :, 2 * dim :].astype(F32)
+        spots = lax.broadcasted_iota(jnp.int32, (toks, width), 1).astype(F32)
+        quarter = LANES // 4
+        first = jnp.where(meta[:, 0:1] == spots, 1.0, 0.0)
+        second = jnp.where(meta[:, quarter : quarter + 1] == spots, 1.0, 0.0)
+        return first, second, meta
+
+    def stage_tokens(src):
+        @pl.when(src != chip)
+        def _():
+            tok_copy(src, src).wait_recv()
+
+        first, second, meta = picks_of(src)
+        quarter = LANES // 4
+        both = (first + second).T.astype(BF16)
+        step = 512
+        for col in range(0, 2 * dim, step):
+            out = matmul(both, tok[src, :, col : col + step], ((1,), (0,)))
+            sendbuf[src, :, col : col + step] = out.astype(BF16)
+        w0 = jnp.broadcast_to(meta[:, 2 * quarter : 2 * quarter + 1], (toks, LANES)).astype(BF16)
+        w1 = jnp.broadcast_to(meta[:, 3 * quarter : 3 * quarter + 1], (toks, LANES)).astype(BF16)
+        out = matmul(first.T.astype(BF16), w0, ((1,), (0,))) + matmul(
+            second.T.astype(BF16), w1, ((1,), (0,))
+        )
+        sendbuf[src, :, 2 * dim :] = out.astype(BF16)
+        for p in range(1, n_expert):
+            xy_copy(src, expert_peer(p), me_e).start()
+        rows[src * CORES + core, chunk(me_e), :] = sendbuf[src, chunk(me_e), :]
+        sib_copy(src, me_e, core).start()
+
+    def compute(g, extra):
+        weight = rows[g, :, 2 * dim : 2 * dim + 1].astype(F32)
+        inner = jnp.zeros((width, 1), F32)
+        tile = 256
+        for col in range(0, units, tile):
+            cols = slice(col, col + tile)
+            pre = matmul(rows[g, :, :dim], w_in_ref[:, cols], ((1,), (0,)))
+            pre = pre + b_in_ref[:, cols].astype(F32)
+            back = matmul(rows[g, :, dim : 2 * dim], w_out_ref[cols, :], ((1,), (1,)))
+            hidden32, slope = gelu_parts(pre)
+            inner = inner + jnp.sum(hidden32 * back, axis=1, keepdims=True)
+            hid[g, :, cols] = hidden32.astype(BF16)
+            dpre[g, :, cols] = (weight * back * slope).astype(BF16)
+        grads = rows[g, :, dim : 2 * dim].astype(F32)
+        dout[g] = (weight * grads).astype(BF16)
+        bias = jnp.sum(grads * b_out_ref[...].astype(F32), axis=1, keepdims=True)
+        inner = inner + bias * extra
+        for col in range(0, dim, 512):
+            out = matmul(dpre[g], w_in_ref[col : col + 512, :], ((1,), (1,)))
+            dx[g, :, col : col + 512] = out.astype(BF16)
+        dx[g, :, dim:] = split_pair(inner, width)
+
+    def stage_rows(src):
+        for p in range(1, n_expert):
+            peer = expert_peer(p)
+            xy_copy(src, peer, peer).wait_recv()
+            sib_copy(src, peer, core).start()
+        compute(src * CORES + core, jnp.where(src == chip, 1.0, 0.0))
+
+    def stage_sibling(src):
+        for e in range(n_expert):
+            sib_copy(src, e, 1 - core).wait_recv()
+        compute(src * CORES + 1 - core, 0.0)
+        dx_copy(src, 1 - core).start()
+
+    def stage_return(src):
+        dx_copy(src, core).wait_recv()
+        g = src * CORES + core
+        total = dx[g, :, :dim].astype(F32) + dxrecv[src, :, :dim].astype(F32)
+        retsend[src, :, :dim] = total.astype(BF16)
+        pair = join_pair(dx[g, :, dim:]) + join_pair(dxrecv[src, :, dim:])
+        retsend[src, :, dim:] = split_pair(pair, width)
+        for p in range(1, n_expert):
+            ret_copy(src, expert_peer(p), me_e).start()
+        retrecv[src, chunk(me_e), :] = retsend[src, chunk(me_e), :]
+
+    def stage_combine(src):
+        for p in range(1, n_expert):
+            peer = expert_peer(p)
+            ret_copy(src, peer, peer).wait_recv()
+        first, second, _ = picks_of(src)
+        both = (first + second).astype(BF16)
+        grads = matmul(both, retrecv[src, :, :dim], ((1,), (0,)))
+        ext = retrecv[src, :, dim:]
+        one = join_pair(matmul(first.astype(BF16), ext, ((1,), (0,))))
+        two = join_pair(matmul(second.astype(BF16), ext, ((1,), (0,))))
+
+        @pl.when(src == chip)
+        def _():
+            facc[:, :dim] = grads
+            facc[:, dim : dim + LANES] = jnp.broadcast_to(one, (toks, LANES))
+            facc[:, dim + LANES :] = jnp.broadcast_to(two, (toks, LANES))
+
+        @pl.when(src != chip)
+        def _():
+            fsend[src, :, :dim] = grads.astype(BF16)
+            fsend[src, :, dim : dim + LANES] = split_pair(one, toks)
+            fsend[src, :, dim + LANES :] = split_pair(two, toks)
+            fin_copy(src, chip).start()
+
+    barrier = pltpu.get_barrier_semaphore()
+
+    def greet(device):
+        pl.semaphore_signal(
+            barrier, inc=1, device_id=device, device_id_type=pl.DeviceIdType.MESH
+        )
+
+    for p in range(1, n_expert):
+        greet((expert_peer(p), me_z))
+    for p in range(1, chips):
+        greet((me_e, chip_peer(p) * CORES + core))
+    greet(sibling)
+    tok[chip] = pay_ref[...]
+    pl.semaphore_wait(barrier, n_expert + chips - 1)
+
+    for p in range(1, chips):
+        tok_copy(chip_peer(p), chip).start()
+
+    @pl.loop(0, chips + 2)
+    def _(step):
+        @pl.when(step < chips)
+        def _():
+            stage_tokens(order(step))
+
+        @pl.when((step >= 1) & (step < chips + 1))
+        def _():
+            stage_rows(order(step - 1))
+
+        @pl.when(step >= 2)
+        def _():
+            stage_sibling(order(step - 2))
+
+        @pl.when(step >= 3)
+        def _():
+            stage_return(order(step - 3))
+
+        @pl.when(step >= 4)
+        def _():
+            stage_combine(order(step - 4))
+
+    stage_return(order(chips - 1))
+    groups = chips * CORES
+    all_rows = groups * width
+    d_all = dpre[...].reshape(all_rows, units)
+    for col in range(0, dim, 256):
+        x_all = rows[:, :, col : col + 256].reshape(all_rows, 256)
+        gwi_ref[col : col + 256, :] = matmul(x_all, d_all, ((0,), (0,))).astype(BF16)
+    stage_combine(order(chips - 2))
+    stage_combine(order(chips - 1))
+    o_all = dout[...].reshape(all_rows, dim)
+    for col in range(0, units, 256):
+        h_all = hid[:, :, col : col + 256].reshape(all_rows, 256)
+        gwo_ref[col : col + 256, :] = matmul(h_all, o_all, ((0,), (0,))).astype(BF16)
+    ones = jnp.ones((8, all_rows), BF16)
+    gbi_ref[...] = matmul(ones, d_all, ((1,), (0,)))[0:1]
+    gbo_ref[...] = matmul(ones, o_all, ((1,), (0,)))[0:1]
+
+    total = facc[:, :dim]
+    one = facc[:, dim : dim + 1]
+    two = facc[:, dim + LANES : dim + LANES + 1]
+    for p in range(1, chips):
+        other = chip_peer(p)
+        fin_copy(other, other).wait_recv()
+        total = total + frecv[other, :, :dim].astype(F32)
+        one = one + join_pair(frecv[other, :, dim : dim + LANES])
+        two = two + join_pair(frecv[other, :, dim + LANES :])
+    gt_ref[...] = total.astype(BF16)
+    gc_ref[:, 0:1] = one
+    gc_ref[:, 1:2] = two
+
+    for p in range(1, chips):
+        other = chip_peer(p)
+        tok_copy(other, chip).wait_send()
+        fin_copy(other, chip).wait_send()
+    for src in range(chips):
+        for p in range(1, n_expert):
+            xy_copy(src, expert_peer(p), me_e).wait_send()
+            ret_copy(src, expert_peer(p), me_e).wait_send()
+        for e in range(n_expert):
+            sib_copy(src, e, core).wait_send()
+        dx_copy(src, 1 - core).wait_send()
+
+
+def scratch_sizes(n_expert, chips, cap, toks, dim, units):
+    width, groups = n_expert * cap, chips * CORES
+    return [
+        ((chips, toks, 2 * dim + LANES), BF16),
+        ((chips, width, 2 * dim + LANES), BF16),
+        ((groups, width, 2 * dim + LANES), BF16),
+        ((groups, width, units), BF16),
+        ((groups, width, units), BF16),
+        ((groups, width, dim), BF16),
+        ((groups, width, dim + LANES), BF16),
+        ((chips, width, dim + LANES), BF16),
+        ((chips, width, dim + LANES), BF16),
+        ((chips, width, dim + LANES), BF16),
+        ((chips, toks, dim + 2 * LANES), BF16),
+        ((chips, toks, dim + 2 * LANES), BF16),
+        ((toks, dim + 2 * LANES), F32),
+    ]
+
+
+def on_device(tokens, grads_out, routes, slots, combine, w_in, b_in, w_out, b_out):
+    n_expert = lax.axis_size("expert")
+    n_zero = lax.axis_size("zero")
+    toks, dim = tokens.shape
+    units = w_in.shape[2]
+    cap = TOP * toks // n_expert
+    chips = n_zero // CORES
+    sizes = scratch_sizes(n_expert, chips, cap, toks, dim, units)
+    held = sum(functools.reduce(lambda a, b: a * b, s) * jnp.dtype(t).itemsize for s, t in sizes)
+    if held > (46 << 20) or n_expert * cap > 256 or n_zero % CORES or chips < 3:
+        return plain_device(
+            tokens, grads_out, routes, slots, combine, w_in, b_in, w_out, b_out
+        )
+    places = jnp.where(slots < cap, routes * cap + slots, -1).astype(BF16)
+    meta = jnp.repeat(jnp.concatenate([places, combine], axis=1), LANES // 4, axis=1)
+    payload = jnp.concatenate([tokens, grads_out, meta], axis=1)
+    vmem = pl.BlockSpec(memory_space=pltpu.VMEM)
+    sem = pltpu.SemaphoreType.DMA
+    outs = pl.pallas_call(
+        functools.partial(fused_kernel, n_expert, chips, cap),
+        out_shape=(
+            jax.ShapeDtypeStruct((toks, dim), BF16),
+            jax.ShapeDtypeStruct((toks, TOP), F32),
+            jax.ShapeDtypeStruct((dim, units), BF16),
+            jax.ShapeDtypeStruct((1, units), F32),
+            jax.ShapeDtypeStruct((units, dim), BF16),
+            jax.ShapeDtypeStruct((1, dim), F32),
+        ),
+        in_specs=[vmem] * 5,
+        out_specs=(vmem,) * 6,
+        scratch_shapes=[pltpu.VMEM(s, t) for s, t in sizes]
+        + [
+            sem((chips,)), sem((chips,)),
+            sem((chips, n_expert)), sem((chips, n_expert)),
+            sem((chips, n_expert)), sem((chips, n_expert)),
+            sem((chips,)), sem((chips,)),
+            sem((chips, n_expert)), sem((chips, n_expert)),
+            sem((chips,)), sem((chips,)),
+        ],
+        compiler_params=pltpu.CompilerParams(
+            collective_id=0, has_side_effects=True, vmem_limit_bytes=60 << 20
+        ),
+        name="routed_expert_backward",
+    )(payload, w_in[0], b_in, w_out[0], b_out)
+    gt, gc, gwi, gbi, gwo, gbo = outs
+    return (gt, gc, gwi[None], gbi, gwo[None], gbo)
+
+
 def solution(mesh):
     in_specs = (
         P(("expert", "zero"), None),

time: 272 us -> 147 us (0.54)
  waiting for transfers between devices: 173 us -> 0 us
  Pallas kernels: 0 us -> 135 us
  matrix products: 34.1 us -> 0 us
  blocking collectives: 20.1 us -> 0 us
  starting transfers between devices: 16.4 us -> 0 us
  between operations: 14.2 us -> 0.65 us
  other arithmetic: 12.5 us -> 3.25 us
  local copies, waits for them, and re-layouts: 1.39 us -> 7.77 us
    pallas_call x0 -> x1, Pallas kernels: none -> 135 us  [on_device(): pl.pallas_call(functools.partial(fused_kernel, n_expert, chips, cap), out...]
    all_to_all x4 -> x0, waiting for transfers between devices: 87 us -> none  [the longest x1 85.1 us: on_device(): lax.all_to_all(slot_dx.reshape(n_zero, width, dim), 'zero', split_axis=0,...]
    all_gather x1 -> x0, waiting for transfers between devices: 86.1 us -> none  [on_device(): rows = lax.all_gather(got, 'zero', axis=0, tiled=True)]
    dot_general x8 -> x0, matrix products: 34.1 us -> none  [the longest x1 7.1 us: on_device(): jnp.einsum('ra,rb->ab', hidden, dout, preferred_element_type=f32)]
    all_to_all x1 -> x0, blocking collectives: 20.1 us -> none  [on_device(): lax.all_to_all(send.reshape(n_expert, cap_rows, -1), 'expert', split_axis...]
    all_to_all x4 -> x0, starting transfers between devices: 16.4 us -> none  [the longest x1 5.16 us: on_device(): lax.all_to_all(slot_dx.reshape(n_zero, width, dim), 'zero', split_axis=0,...]
    reduce_sum x5 -> x0, other arithmetic: 9.36 us -> none  [the longest x1 4.05 us: on_device(): sum_dx = jnp.sum(part_dx.astype(f32), axis=0).astype(bf16)]
    unnamed x14 -> x12, local copies, waits for them, and re-layouts: 0.03 us -> 7.65 us
  transfers between devices with their start and end apart: 5 -> 0, of which waited for: 3 -> 0; matrix products, arithmetic and copies ran while one was open for 11% -> 0% of each run, Pallas kernels for 0% -> 0%
where the time goes in v2:
time: 147 us
  Pallas kernels  135 us (92%)
  local copies, waits for them, and re-layouts  7.77 us (5%)
  other arithmetic  3.25 us (2%)
    pallas_call x1, Pallas kernels, on_device(): pl.pallas_call(functools.partial(fused_kernel, n_expert, chips, cap), out...  135 us
    unnamed x12, local copies, waits for them, and re-layouts  7.65 us

profile of v2, /device:TPU:0, one launch (start us, length us, event | category | flops | bytes accessed | tf_op | source)
XLA Modules:
  0.0 147.0 jit_solution(503352474928806711)
XLA Ops:
  0.6 0.7 fusion
  1.3 0.7 pad_maximum_fusion.1
  2.0 0.1 copy.17
  2.1 1.9 %pad_maximum_fusion.pay_ref = bf16[128,2176]{1,0:T(8,128)(2,1)} fusion(bf16[128,128]{1,0:T(8,128)(2,1)S(1)} %copy.17, bf16[128,1024]{1,0:T(8,128)(2,1)} %param.10, bf16[128,1024]{1,0:T(8,128)(2,1)} %param.9), kind=kLoop, calls=%fused_computation | loop fusion | flops 1671168 | bytes 1114112 | tf_op jit(solution)/shard_map/concatenate | solution.py:386
  4.0 135.4 %routed_expert_backward.1 = (bf16[128,1024]{1,0:T(8,128)(2,1)}, f32[128,2]{1,0:T(8,128)}, bf16[1024,512]{1,0:T(8,128)(2,1)}, f32[1,512]{1,0:T(1,128)}, bf16[512,1024]{1,0:T(8,128)(2,1)}, /*index=5*/f32[1,1024]{1,0:T(1,128)}) custom-call(bf16[128,2176]{1,0:T(8,128)(2,1)} %pad_maximum_fusion.pay_ref, bf16[1024,512]{1,0:T(8,128)(2,1)} %bitcast.5, ...), custom_call_target="tpu_custom_call" | custom-call | tf_op jit(solution)/shard_map/routed_expert_backward/pallas_call | solution.py:389
  139.4 1.5 %copy.18 = f32[128,2]{0,1:T(2,128)} copy(f32[128,2]{1,0:T(8,128)} %get-tuple-element.25) | data formatting | bytes 2048
  140.9 1.7 %copy.24 = bf16[128,1024]{1,0:T(8,128)(2,1)} copy(bf16[128,1024]{1,0:T(8,128)(2,1)} %get-tuple-element.36) | data formatting | bytes 524288
  142.5 0.0 copy-start.2
  142.5 0.0 copy-start
  142.5 2.4 %copy.25 = bf16[1,1024,512]{2,1,0:T(8,128)(2,1)} copy(bf16[1,1024,512]{2,1,0:T(8,128)(2,1)} %bitcast.8) | data formatting | bytes 2097152
  144.9 0.0 copy-done.2
  144.9 0.6 copy.26
  145.5 0.0 copy-done
  145.5 0.0 copy-start.1
  145.5 1.0 copy.27
  146.4 0.0 copy-done.1
  146.4 0.6 copy.28
  (1 shorter events, 0.0 us)
Async XLA Ops:
  142.5 2.4 %copy-start.2 = (f32[1,512]{1,0:T(1,128)S(1)}, f32[1,512]{1,0:T(1,128)}, u32[]{:S(2)}) copy-start(f32[1,512]{1,0:T(1,128)} %get-tuple-element.39) | copy-start | bytes 6148
  142.5 2.9 %copy-start = (bf16[512,1024]{1,0:T(8,128)(2,1)S(1)}, bf16[512,1024]{1,0:T(8,128)(2,1)}, u32[]{:S(2)}) copy-start(bf16[512,1024]{1,0:T(8,128)(2,1)} %get-tuple-element.16) | copy-start | bytes 3145732
  145.5 1.0 copy-start.1

commit v3 on v2

--- a/solution.py
+++ b/solution.py
@@ -94,7 +94,7 @@
 
 
 def fused_kernel(
-    n_expert, chips, cap, pay_ref, w_in_ref, b_in_ref, w_out_ref, b_out_ref,
+    n_expert, chips, cap, x_ref, g_ref, meta_ref, w_in_ref, b_in_ref, w_out_ref, b_out_ref,
     gt_ref, gc_ref, gwi_ref, gbi_ref, gwo_ref, gbo_ref,
     tok, sendbuf, rows, hid, dpre, dout, dx, dxrecv, retsend, retrecv, fsend, frecv, facc,
     tok_s, tok_r, xy_s, xy_r, sib_s, sib_r, dx_s, dx_r, ret_s, ret_r, fin_s, fin_r,
@@ -132,10 +132,29 @@
             device_id_type=pl.DeviceIdType.MESH,
         )
 
-    def tok_copy(to, frm):
-        return remote(
-            tok.at[frm], tok.at[frm], tok_s.at[to], tok_r.at[frm], (me_e, to * CORES + core)
-        )
+    def tok_copy(src, way):
+        to = chip + (1 if way else -1)
+        return remote(
+            tok.at[src], tok.at[src], tok_s.at[way, src], tok_r.at[src],
+            (me_e, to * CORES + core),
+        )
+
+    def pass_tokens(away):
+        @pl.when(chip >= away)
+        def _():
+            tok_copy(chip - away, 1).wait_recv()
+
+            @pl.when(chip < chips - 1)
+            def _():
+                tok_copy(chip - away, 1).start()
+
+        @pl.when(chip + away < chips)
+        def _():
+            tok_copy(chip + away, 0).wait_recv()
+
+            @pl.when(chip > 0)
+            def _():
+                tok_copy(chip + away, 0).start()
 
     def xy_copy(src, peer, frm):
         return remote(
@@ -174,10 +193,6 @@
         return first, second, meta
 
     def stage_tokens(src):
-        @pl.when(src != chip)
-        def _():
-            tok_copy(src, src).wait_recv()
-
         first, second, meta = picks_of(src)
         quarter = LANES // 4
         both = (first + second).T.astype(BF16)
@@ -278,42 +293,48 @@
     for p in range(1, chips):
         greet((me_e, chip_peer(p) * CORES + core))
     greet(sibling)
-    tok[chip] = pay_ref[...]
+    tok[chip, :, :dim] = x_ref[...]
+    tok[chip, :, dim : 2 * dim] = g_ref[...]
+    tok[chip, :, 2 * dim :] = meta_ref[...]
     pl.semaphore_wait(barrier, n_expert + chips - 1)
 
-    for p in range(1, chips):
-        tok_copy(chip_peer(p), chip).start()
-
-    @pl.loop(0, chips + 2)
+    @pl.when(chip < chips - 1)
+    def _():
+        tok_copy(chip, 1).start()
+
+    @pl.when(chip > 0)
+    def _():
+        tok_copy(chip, 0).start()
+
+    @pl.loop(0, chips + 1)
     def _(step):
+        @pl.when((step >= 1) & (step < chips))
+        def _():
+            pass_tokens(step)
+
         @pl.when(step < chips)
         def _():
             stage_tokens(order(step))
 
-        @pl.when((step >= 1) & (step < chips + 1))
+        @pl.when(step >= 1)
         def _():
             stage_rows(order(step - 1))
+            stage_sibling(order(step - 1))
 
         @pl.when(step >= 2)
         def _():
-            stage_sibling(order(step - 2))
-
-        @pl.when(step >= 3)
-        def _():
-            stage_return(order(step - 3))
-
-        @pl.when(step >= 4)
-        def _():
-            stage_combine(order(step - 4))
-
-    stage_return(order(chips - 1))
+            stage_combine(order(step - 2))
+
+        @pl.when(step >= 1)
+        def _():
+            stage_return(order(step - 1))
+
     groups = chips * CORES
     all_rows = groups * width
     d_all = dpre[...].reshape(all_rows, units)
     for col in range(0, dim, 256):
         x_all = rows[:, :, col : col + 256].reshape(all_rows, 256)
         gwi_ref[col : col + 256, :] = matmul(x_all, d_all, ((0,), (0,))).astype(BF16)
-    stage_combine(order(chips - 2))
     stage_combine(order(chips - 1))
     o_all = dout[...].reshape(all_rows, dim)
     for col in range(0, units, 256):
@@ -338,9 +359,16 @@
 
     for p in range(1, chips):
         other = chip_peer(p)
-        tok_copy(other, chip).wait_send()
         fin_copy(other, chip).wait_send()
     for src in range(chips):
+        @pl.when((src <= chip) & (chip < chips - 1))
+        def _():
+            tok_copy(src, 1).wait_send()
+
+        @pl.when((src >= chip) & (chip > 0))
+        def _():
+            tok_copy(src, 0).wait_send()
+
         for p in range(1, n_expert):
             xy_copy(src, expert_peer(p), me_e).wait_send()
             ret_copy(src, expert_peer(p), me_e).wait_send()
@@ -383,7 +411,6 @@
         )
     places = jnp.where(slots < cap, routes * cap + slots, -1).astype(BF16)
     meta = jnp.repeat(jnp.concatenate([places, combine], axis=1), LANES // 4, axis=1)
-    payload = jnp.concatenate([tokens, grads_out, meta], axis=1)
     vmem = pl.BlockSpec(memory_space=pltpu.VMEM)
     sem = pltpu.SemaphoreType.DMA
     outs = pl.pallas_call(
@@ -396,11 +423,11 @@
             jax.ShapeDtypeStruct((units, dim), BF16),
             jax.ShapeDtypeStruct((1, dim), F32),
         ),
-        in_specs=[vmem] * 5,
+        in_specs=[vmem] * 7,
         out_specs=(vmem,) * 6,
         scratch_shapes=[pltpu.VMEM(s, t) for s, t in sizes]
         + [
-            sem((chips,)), sem((chips,)),
+            sem((2, chips)), sem((chips,)),
             sem((chips, n_expert)), sem((chips, n_expert)),
             sem((chips, n_expert)), sem((chips, n_expert)),
             sem((chips,)), sem((chips,)),
@@ -411,7 +438,7 @@
             collective_id=0, has_side_effects=True, vmem_limit_bytes=60 << 20
         ),
         name="routed_expert_backward",
-    )(payload, w_in[0], b_in, w_out[0], b_out)
+    )(tokens, grads_out, meta, w_in[0], b_in, w_out[0], b_out)
     gt, gc, gwi, gbi, gwo, gbo = outs
     return (gt, gc, gwi[None], gbi, gwo[None], gbo)
 

time: 147 us -> 120 us (0.82)
  Pallas kernels: 135 us -> 110 us
  other arithmetic: 3.25 us -> 0.02 us
  local copies, waits for them, and re-layouts: 7.77 us -> 9.71 us
    pallas_call x1, Pallas kernels: 135 us -> 110 us  [on_device(): pl.pallas_call(functools.partial(fused_kernel, n_expert, chips, cap), out...]
    concatenate x1 -> x0, other arithmetic: 1.89 us -> none  [on_device(): payload = jnp.concatenate([tokens, grads_out, meta], axis=1)]
    unnamed x12 -> x18, local copies, waits for them, and re-layouts: 7.65 us -> 8.97 us
where the time goes in v3:
time: 120 us
  Pallas kernels  110 us (92%)
  local copies, waits for them, and re-layouts  9.71 us (8%)
    pallas_call x1, Pallas kernels, on_device(): pl.pallas_call(functools.partial(fused_kernel, n_expert, chips, cap), out...  110 us
    unnamed x18, local copies, waits for them, and re-layouts  8.97 us

profile of v3, /device:TPU:0, one launch (start us, length us, event | category | flops | bytes accessed | tf_op | source)
XLA Modules:
  0.0 120.2 jit_solution(13814420706004131146)
XLA Ops:
  0.6 0.0 copy-start.4
  0.6 0.0 copy-start.3
  0.7 0.7 copy-done.4
  1.3 0.0 copy-done.3
  1.3 0.0 copy-start.5
  1.3 0.6 copy-done.5
  2.0 0.7 copy.17.meta_ref
  2.7 109.8 %routed_expert_backward.1 = (bf16[128,1024]{1,0:T(8,128)(2,1)}, f32[128,2]{1,0:T(8,128)}, bf16[1024,512]{1,0:T(8,128)(2,1)}, f32[1,512]{1,0:T(1,128)}, bf16[512,1024]{1,0:T(8,128)(2,1)}, /*index=5*/f32[1,1024]{1,0:T(1,128)}) custom-call(bf16[128,1024]{1,0:T(8,128)(2,1)} %x_ref.1, bf16[128,1024]{1,0:T(8,128)(2,1)} %g_ref.1, bf16[128,128]{1,0:T(8,128)(2,1)} %copy.17.meta_ref, ...), custom_call_target="tpu_custom_call" | custom-call | tf_op jit(solution)/shard_map/routed_expert_backward/pallas_call | solution.py:416
  112.5 1.5 %copy.18 = f32[128,2]{0,1:T(2,128)} copy(f32[128,2]{1,0:T(8,128)} %get-tuple-element.25) | data formatting | bytes 2048
  114.0 1.7 %copy.24 = bf16[128,1024]{1,0:T(8,128)(2,1)} copy(bf16[128,1024]{1,0:T(8,128)(2,1)} %get-tuple-element.36) | data formatting | bytes 524288
  115.7 0.0 copy-start.2
  115.7 0.0 copy-start
  115.7 2.4 %copy.25 = bf16[1,1024,512]{2,1,0:T(8,128)(2,1)} copy(bf16[1,1024,512]{2,1,0:T(8,128)(2,1)} %bitcast.8) | data formatting | bytes 2097152
  118.0 0.0 copy-done.2
  118.0 0.6 copy.26
  118.6 0.0 copy-done
  118.6 0.0 copy-start.1
  118.6 1.0 copy.27
  119.6 0.0 copy-done.1
  119.6 0.6 copy.28
  (3 shorter events, 0.0 us)
Async XLA Ops:
  0.6 0.7 copy-start.4
  0.6 0.7 copy-start.3
  1.3 0.7 copy-start.5
  115.7 2.4 %copy-start.2 = (f32[1,512]{1,0:T(1,128)S(1)}, f32[1,512]{1,0:T(1,128)}, u32[]{:S(2)}) copy-start(f32[1,512]{1,0:T(1,128)} %get-tuple-element.39) | copy-start | bytes 6148
  115.7 2.9 %copy-start = (bf16[512,1024]{1,0:T(8,128)(2,1)S(1)}, bf16[512,1024]{1,0:T(8,128)(2,1)}, u32[]{:S(2)}) copy-start(bf16[512,1024]{1,0:T(8,128)(2,1)} %get-tuple-element.16) | copy-start | bytes 3145732
  118.6 1.0 copy-start.1

commit v4 on v3

--- a/solution.py
+++ b/solution.py
@@ -94,10 +94,10 @@
 
 
 def fused_kernel(
-    n_expert, chips, cap, x_ref, g_ref, meta_ref, w_in_ref, b_in_ref, w_out_ref, b_out_ref,
-    gt_ref, gc_ref, gwi_ref, gbi_ref, gwo_ref, gbo_ref,
-    tok, sendbuf, rows, hid, dpre, dout, dx, dxrecv, retsend, retrecv, fsend, frecv, facc,
-    tok_s, tok_r, xy_s, xy_r, sib_s, sib_r, dx_s, dx_r, ret_s, ret_r, fin_s, fin_r,
+    n_expert, chips, cap, x_hbm, g_hbm, meta_hbm, w_in_hbm, b_in_ref, w_out_hbm, b_out_ref,
+    gt_ref, gc_ref, gwi_hbm, gbi_ref, gwo_hbm, gbo_ref,
+    w_in_ref, w_out_ref, gwi_ref, gwo_ref, tok, sendbuf, rows, hid, dpre, dout, dx, dxrecv, retsend, retrecv, fsend, frecv, facc,
+    tok_s, tok_r, xy_s, xy_r, sib_s, sib_r, dx_s, dx_r, ret_s, ret_r, fin_s, fin_r, loc,
 ):
     me_e = lax.axis_index("expert")
     me_z = lax.axis_index("zero")
@@ -211,51 +211,59 @@
         rows[src * CORES + core, chunk(me_e), :] = sendbuf[src, chunk(me_e), :]
         sib_copy(src, me_e, core).start()
 
-    def compute(g, extra):
-        weight = rows[g, :, 2 * dim : 2 * dim + 1].astype(F32)
-        inner = jnp.zeros((width, 1), F32)
-        tile = 256
-        for col in range(0, units, tile):
-            cols = slice(col, col + tile)
-            pre = matmul(rows[g, :, :dim], w_in_ref[:, cols], ((1,), (0,)))
-            pre = pre + b_in_ref[:, cols].astype(F32)
-            back = matmul(rows[g, :, dim : 2 * dim], w_out_ref[cols, :], ((1,), (1,)))
-            hidden32, slope = gelu_parts(pre)
-            inner = inner + jnp.sum(hidden32 * back, axis=1, keepdims=True)
-            hid[g, :, cols] = hidden32.astype(BF16)
-            dpre[g, :, cols] = (weight * back * slope).astype(BF16)
-        grads = rows[g, :, dim : 2 * dim].astype(F32)
-        dout[g] = (weight * grads).astype(BF16)
-        bias = jnp.sum(grads * b_out_ref[...].astype(F32), axis=1, keepdims=True)
-        inner = inner + bias * extra
-        for col in range(0, dim, 512):
-            out = matmul(dpre[g], w_in_ref[col : col + 512, :], ((1,), (1,)))
-            dx[g, :, col : col + 512] = out.astype(BF16)
-        dx[g, :, dim:] = split_pair(inner, width)
-
     def stage_rows(src):
         for p in range(1, n_expert):
             peer = expert_peer(p)
             xy_copy(src, peer, peer).wait_recv()
             sib_copy(src, peer, core).start()
-        compute(src * CORES + core, jnp.where(src == chip, 1.0, 0.0))
-
-    def stage_sibling(src):
         for e in range(n_expert):
             sib_copy(src, e, 1 - core).wait_recv()
-        compute(src * CORES + 1 - core, 0.0)
+
+    def stage_compute(src):
+        pair = pl.ds(src * CORES, CORES)
+        both = CORES * width
+        weight = rows[pair, :, 2 * dim :].reshape(both, LANES).astype(F32)[:, 0:1]
+        inner = jnp.zeros((both, 1), F32)
+        tile = 256
+        for col in range(0, units, tile):
+            cols = slice(col, col + tile)
+            x = rows[pair, :, :dim].reshape(both, dim)
+            pre = matmul(x, w_in_ref[:, cols], ((1,), (0,)))
+            pre = pre + b_in_ref[:, cols].astype(F32)
+            g = rows[pair, :, dim : 2 * dim].reshape(both, dim)
+            back = matmul(g, w_out_ref[cols, :], ((1,), (1,)))
+            hidden32, slope = gelu_parts(pre)
+            inner = inner + jnp.sum(hidden32 * back, axis=1, keepdims=True)
+            hid[pair, :, cols] = hidden32.astype(BF16).reshape(CORES, width, tile)
+            dpre[pair, :, cols] = (weight * back * slope).astype(BF16).reshape(CORES, width, tile)
+        for col in range(0, dim, 512):
+            d = dpre[pair].reshape(both, units)
+            out = matmul(d, w_in_ref[col : col + 512, :], ((1,), (1,)))
+            dx[pair, :, col : col + 512] = out.astype(BF16).reshape(CORES, width, 512)
+        dx[pair, :, dim:] = split_pair(inner, both).reshape(CORES, width, LANES)
         dx_copy(src, 1 - core).start()
 
     def stage_return(src):
+        for lane in range(CORES):
+            g = src * CORES + lane
+            weight = rows[g, :, 2 * dim :].astype(F32)[:, 0:1]
+            dout[g] = (weight * rows[g, :, dim : 2 * dim].astype(F32)).astype(BF16)
+        g = src * CORES + core
+        grads = rows[g, :, dim : 2 * dim].astype(F32)
+        bias = jnp.sum(grads * b_out_ref[...].astype(F32), axis=1, keepdims=True)
+        bias = bias * jnp.where(src == chip, 1.0, 0.0)
         dx_copy(src, core).wait_recv()
-        g = src * CORES + core
         total = dx[g, :, :dim].astype(F32) + dxrecv[src, :, :dim].astype(F32)
         retsend[src, :, :dim] = total.astype(BF16)
-        pair = join_pair(dx[g, :, dim:]) + join_pair(dxrecv[src, :, dim:])
+        pair = join_pair(dx[g, :, dim:]) + join_pair(dxrecv[src, :, dim:]) + bias
         retsend[src, :, dim:] = split_pair(pair, width)
         for p in range(1, n_expert):
             ret_copy(src, expert_peer(p), me_e).start()
         retrecv[src, chunk(me_e), :] = retsend[src, chunk(me_e), :]
+
+    def in_halves(one, two):
+        lane = lax.broadcasted_iota(jnp.int32, (toks, LANES), 1)
+        return jnp.where(lane < LANES // 2, one, two)
 
     def stage_combine(src):
         for p in range(1, n_expert):
@@ -271,14 +279,15 @@
         @pl.when(src == chip)
         def _():
             facc[:, :dim] = grads
-            facc[:, dim : dim + LANES] = jnp.broadcast_to(one, (toks, LANES))
-            facc[:, dim + LANES :] = jnp.broadcast_to(two, (toks, LANES))
+            facc[:, dim:] = in_halves(one, two)
 
         @pl.when(src != chip)
         def _():
             fsend[src, :, :dim] = grads.astype(BF16)
-            fsend[src, :, dim : dim + LANES] = split_pair(one, toks)
-            fsend[src, :, dim + LANES :] = split_pair(two, toks)
+            high = in_halves(one, two).astype(BF16).astype(F32)
+            odd = lax.broadcasted_iota(jnp.int32, (toks, LANES), 1) % 2
+            ext = jnp.where(odd == 0, high, in_halves(one, two) - high)
+            fsend[src, :, dim:] = ext.astype(BF16)
             fin_copy(src, chip).start()
 
     barrier = pltpu.get_barrier_semaphore()
@@ -293,9 +302,20 @@
     for p in range(1, chips):
         greet((me_e, chip_peer(p) * CORES + core))
     greet(sibling)
-    tok[chip, :, :dim] = x_ref[...]
-    tok[chip, :, dim : 2 * dim] = g_ref[...]
-    tok[chip, :, 2 * dim :] = meta_ref[...]
+    loads = [
+        pltpu.make_async_copy(src, dst, loc.at[i])
+        for i, (src, dst) in enumerate((
+            (x_hbm, tok.at[chip, :, :dim]),
+            (g_hbm, tok.at[chip, :, dim : 2 * dim]),
+            (meta_hbm, tok.at[chip, :, 2 * dim :]),
+            (w_in_hbm, w_in_ref),
+            (w_out_hbm, w_out_ref),
+        ))
+    ]
+    for load in loads:
+        load.start()
+    for load in loads[:3]:
+        load.wait()
     pl.semaphore_wait(barrier, n_expert + chips - 1)
 
     @pl.when(chip < chips - 1)
@@ -316,46 +336,66 @@
         def _():
             stage_tokens(order(step))
 
+        @pl.when(step == 0)
+        def _():
+            for load in loads[3:]:
+                load.wait()
+
         @pl.when(step >= 1)
         def _():
             stage_rows(order(step - 1))
-            stage_sibling(order(step - 1))
+            stage_compute(order(step - 1))
+            stage_return(order(step - 1))
 
         @pl.when(step >= 2)
         def _():
             stage_combine(order(step - 2))
-
-        @pl.when(step >= 1)
-        def _():
-            stage_return(order(step - 1))
 
     groups = chips * CORES
     all_rows = groups * width
-    d_all = dpre[...].reshape(all_rows, units)
-    for col in range(0, dim, 256):
-        x_all = rows[:, :, col : col + 256].reshape(all_rows, 256)
-        gwi_ref[col : col + 256, :] = matmul(x_all, d_all, ((0,), (0,))).astype(BF16)
+
+    def weights_in(first, last):
+        for col in range(first, last, 256):
+            x_all = rows[:, :, col : col + 256].reshape(all_rows, 256)
+            d_all = dpre[...].reshape(all_rows, units)
+            gwi_ref[col : col + 256, :] = matmul(x_all, d_all, ((0,), (0,))).astype(BF16)
+
+    weights_in(0, dim // 2)
     stage_combine(order(chips - 1))
+    weights_in(dim // 2, dim)
+    store_in = pltpu.make_async_copy(gwi_ref, gwi_hbm, loc.at[5])
+    store_in.start()
     o_all = dout[...].reshape(all_rows, dim)
     for col in range(0, units, 256):
         h_all = hid[:, :, col : col + 256].reshape(all_rows, 256)
         gwo_ref[col : col + 256, :] = matmul(h_all, o_all, ((0,), (0,))).astype(BF16)
+    store_out = pltpu.make_async_copy(gwo_ref, gwo_hbm, loc.at[6])
+    store_out.start()
     ones = jnp.ones((8, all_rows), BF16)
-    gbi_ref[...] = matmul(ones, d_all, ((1,), (0,)))[0:1]
+    gbi_ref[...] = matmul(ones, dpre[...].reshape(all_rows, units), ((1,), (0,)))[0:1]
     gbo_ref[...] = matmul(ones, o_all, ((1,), (0,)))[0:1]
 
     total = facc[:, :dim]
-    one = facc[:, dim : dim + 1]
-    two = facc[:, dim + LANES : dim + LANES + 1]
+    ext = facc[:, dim:]
+    one, two = ext[:, 0:1], ext[:, LANES // 2 : LANES // 2 + 1]
+    lane = lax.broadcasted_iota(jnp.int32, (toks, LANES), 1)
     for p in range(1, chips):
         other = chip_peer(p)
         fin_copy(other, other).wait_recv()
         total = total + frecv[other, :, :dim].astype(F32)
-        one = one + join_pair(frecv[other, :, dim : dim + LANES])
-        two = two + join_pair(frecv[other, :, dim + LANES :])
+        ext = frecv[other, :, dim:].astype(F32)
+        scale = 4.0 / LANES
+        one = one + scale * jnp.sum(
+            jnp.where(lane < LANES // 2, ext, 0.0), axis=1, keepdims=True
+        )
+        two = two + scale * jnp.sum(
+            jnp.where(lane < LANES // 2, 0.0, ext), axis=1, keepdims=True
+        )
     gt_ref[...] = total.astype(BF16)
     gc_ref[:, 0:1] = one
     gc_ref[:, 1:2] = two
+    store_in.wait()
+    store_out.wait()
 
     for p in range(1, chips):
         other = chip_peer(p)
@@ -377,9 +417,26 @@
         dx_copy(src, 1 - core).wait_send()
 
 
+def hand_over(a_in, b_in, c_in, a_out, b_out, c_out, sems):
+    copies = []
+    for i, (src, dst) in enumerate(((a_in, a_out), (b_in, b_out), (c_in, c_out))):
+        part = src.shape[0] // 4
+        for j in range(4):
+            at = pl.ds(j * part, part)
+            copies.append(pltpu.make_async_copy(src.at[at], dst.at[at], sems.at[4 * i + j]))
+    for copy in copies:
+        copy.start()
+    for copy in copies:
+        copy.wait()
+
+
 def scratch_sizes(n_expert, chips, cap, toks, dim, units):
     width, groups = n_expert * cap, chips * CORES
     return [
+        ((dim, units), BF16),
+        ((units, dim), BF16),
+        ((dim, units), BF16),
+        ((units, dim), BF16),
         ((chips, toks, 2 * dim + LANES), BF16),
         ((chips, width, 2 * dim + LANES), BF16),
         ((groups, width, 2 * dim + LANES), BF16),
@@ -390,9 +447,9 @@
         ((chips, width, dim + LANES), BF16),
         ((chips, width, dim + LANES), BF16),
         ((chips, width, dim + LANES), BF16),
-        ((chips, toks, dim + 2 * LANES), BF16),
-        ((chips, toks, dim + 2 * LANES), BF16),
-        ((toks, dim + 2 * LANES), F32),
+        ((chips, toks, dim + LANES), BF16),
+        ((chips, toks, dim + LANES), BF16),
+        ((toks, dim + LANES), F32),
     ]
 
 
@@ -412,6 +469,7 @@
     places = jnp.where(slots < cap, routes * cap + slots, -1).astype(BF16)
     meta = jnp.repeat(jnp.concatenate([places, combine], axis=1), LANES // 4, axis=1)
     vmem = pl.BlockSpec(memory_space=pltpu.VMEM)
+    hbm = pl.BlockSpec(memory_space=pl.ANY)
     sem = pltpu.SemaphoreType.DMA
     outs = pl.pallas_call(
         functools.partial(fused_kernel, n_expert, chips, cap),
@@ -423,8 +481,8 @@
             jax.ShapeDtypeStruct((units, dim), BF16),
             jax.ShapeDtypeStruct((1, dim), F32),
         ),
-        in_specs=[vmem] * 7,
-        out_specs=(vmem,) * 6,
+        in_specs=[hbm, hbm, hbm, hbm, vmem, hbm, vmem],
+        out_specs=(vmem, vmem, hbm, vmem, hbm, vmem),
         scratch_shapes=[pltpu.VMEM(s, t) for s, t in sizes]
         + [
             sem((2, chips)), sem((chips,)),
@@ -433,6 +491,7 @@
             sem((chips,)), sem((chips,)),
             sem((chips, n_expert)), sem((chips, n_expert)),
             sem((chips,)), sem((chips,)),
+            sem((7,)),
         ],
         compiler_params=pltpu.CompilerParams(
             collective_id=0, has_side_effects=True, vmem_limit_bytes=60 << 20
@@ -440,6 +499,15 @@
         name="routed_expert_backward",
     )(tokens, grads_out, meta, w_in[0], b_in, w_out[0], b_out)
     gt, gc, gwi, gbi, gwo, gbo = outs
+    gt, gwi, gwo = pl.pallas_call(
+        hand_over,
+        out_shape=tuple(jax.ShapeDtypeStruct(a.shape, a.dtype) for a in (gt, gwi, gwo)),
+        in_specs=[hbm] * 3,
+        out_specs=(hbm,) * 3,
+        scratch_shapes=[sem((12,))],
+        compiler_params=pltpu.CompilerParams(vmem_limit_bytes=60 << 20),
+        name="hand_over",
+    )(gt, gwi, gwo)
     return (gt, gc, gwi[None], gbi, gwo[None], gbo)
 
 

time: 120 us -> 185 us (1.54)
  Pallas kernels: 110 us -> 180 us
  local copies, waits for them, and re-layouts: 9.71 us -> 3.99 us
    pallas_call x0 -> x1, Pallas kernels: none -> 72.7 us  [on_device(): pl.pallas_call(hand_over, out_shape=tuple((jax.ShapeDtypeStruct(a.shape,...]
    unnamed x18 -> x15, local copies, waits for them, and re-layouts: 8.97 us -> 3.26 us
    pallas_call x1, Pallas kernels: 110 us -> 107 us  [on_device(): pl.pallas_call(functools.partial(fused_kernel, n_expert, chips, cap), out...]
where the time goes in v4:
time: 185 us; the launch traced here: 184 us
  Pallas kernels  180 us (97%)
  local copies, waits for them, and re-layouts  3.99 us (2%)
    pallas_call x1, Pallas kernels, on_device(): pl.pallas_call(functools.partial(fused_kernel, n_expert, chips, cap), out...  107 us
    pallas_call x1, Pallas kernels, on_device(): pl.pallas_call(hand_over, out_shape=tuple((jax.ShapeDtypeStruct(a.shape,...  72.7 us

profile of v4, /device:TPU:0, one launch (start us, length us, event | category | flops | bytes accessed | tf_op | source)
XLA Modules:
  0.0 184.3 jit_solution(14426693579164111125)
XLA Ops:
  0.6 0.0 copy-start.4
  0.6 0.0 copy-start.3
  0.7 0.7 copy-done.4
  1.3 0.0 copy-done.3
  1.3 0.0 copy-start.5
  1.3 0.6 copy-done.5
  2.0 0.7 copy.17.meta_hbm
  2.7 106.9 %routed_expert_backward.1 = (bf16[128,1024]{1,0:T(8,128)(2,1)}, f32[128,2]{1,0:T(8,128)}, bf16[1024,512]{1,0:T(8,128)(2,1)}, f32[1,512]{1,0:T(1,128)}, bf16[512,1024]{1,0:T(8,128)(2,1)}, /*index=5*/f32[1,1024]{1,0:T(1,128)}) custom-call(bf16[128,1024]{1,0:T(8,128)(2,1)} %x_hbm.1, bf16[128,1024]{1,0:T(8,128)(2,1)} %g_hbm.1, bf16[128,128]{1,0:T(8,128)(2,1)} %copy.17.meta_hbm, ...), custom_call_target="tpu_custom_call" | custom-call | tf_op jit(solution)/shard_map/routed_expert_backward/pallas_call | solution.py:474
  109.6 0.0 copy-start
  109.6 72.7 %hand_over.1 = (bf16[128,1024]{1,0:T(8,128)(2,1)}, bf16[1024,512]{1,0:T(8,128)(2,1)}, bf16[512,1024]{1,0:T(8,128)(2,1)}) custom-call(bf16[128,1024]{1,0:T(8,128)(2,1)} %get-tuple-element.15.a_in, bf16[1024,512]{1,0:T(8,128)(2,1)} %get-tuple-element.16.b_in, bf16[512,1024]{1,0:T(8,128)(2,1)} %get-tuple-element.17.c_in), custom_call_target="tpu_custom_call" | custom-call | tf_op jit(solution)/shard_map/hand_over/pallas_call | solution.py:502
  182.3 0.0 copy-done
  182.3 0.0 copy-start.2
  182.3 0.6 copy.18
  183.0 0.0 copy-done.2
  183.0 0.0 copy-start.1
  183.0 0.6 copy.21
  183.6 0.1 copy-done.1
  183.7 0.6 copy.22
  (3 shorter events, 0.0 us)
Async XLA Ops:
  0.6 0.7 copy-start.4
  0.6 0.7 copy-start.3
  1.3 0.7 copy-start.5
  109.6 72.7 %copy-start = (f32[128,2]{1,0:T(8,128)S(1)}, f32[128,2]{1,0:T(8,128)}, u32[]{:S(2)}) copy-start(f32[128,2]{1,0:T(8,128)} %get-tuple-element.31) | copy-start | bytes 3076
  182.3 0.7 copy-start.2
  183.0 0.7 copy-start.1

commit v5 on v4

--- a/solution.py
+++ b/solution.py
@@ -97,7 +97,7 @@
     n_expert, chips, cap, x_hbm, g_hbm, meta_hbm, w_in_hbm, b_in_ref, w_out_hbm, b_out_ref,
     gt_ref, gc_ref, gwi_hbm, gbi_ref, gwo_hbm, gbo_ref,
     w_in_ref, w_out_ref, gwi_ref, gwo_ref, tok, sendbuf, rows, hid, dpre, dout, dx, dxrecv, retsend, retrecv, fsend, frecv, facc,
-    tok_s, tok_r, xy_s, xy_r, sib_s, sib_r, dx_s, dx_r, ret_s, ret_r, fin_s, fin_r, loc,
+    tok_s, tok_r, xy_s, xy_r, sib_s, sib_r, dx_s, dx_r, ret_s, ret_r, fin_s, fin_r, loc, part, part_sem,
 ):
     me_e = lax.axis_index("expert")
     me_z = lax.axis_index("zero")
@@ -117,14 +117,12 @@
     def chip_peer(p):
         return lax.rem(chip + p, chips)
 
+    partner = chip + 1 - 2 * (chip % 2)
+    base = chips // 2 * (1 - chip // 2)
+
     def order(step):
-        low = chip
-        high = chips - 1 - chip
-        least = jnp.minimum(low, high)
-        half = (step + 1) // 2
-        near = jnp.where(step % 2 == 1, chip + half, chip - half)
-        far = jnp.where(low < high, step, chips - 1 - step)
-        return jnp.where(step <= 2 * least, near, far)
+        far = jnp.where(chip < chips // 2, step, chips - 1 - step)
+        return jnp.where(step == 0, chip, jnp.where(step == 1, partner, far))
 
     def remote(src, dst, send, recv, device):
         return pltpu.make_async_remote_copy(
@@ -177,6 +175,12 @@
         return remote(
             retsend.at[src, chunk(peer)], retrecv.at[src, chunk(frm)],
             ret_s.at[src, peer], ret_r.at[src, frm], (peer, me_z),
+        )
+
+    def part_copy():
+        return remote(
+            retsend.at[partner], part, part_sem.at[0], part_sem.at[1],
+            (me_e, partner * CORES + core),
         )
 
     def fin_copy(to, frm):
@@ -243,6 +247,19 @@
         dx[pair, :, dim:] = split_pair(inner, both).reshape(CORES, width, LANES)
         dx_copy(src, 1 - core).start()
 
+    def send_return(src):
+        for p in range(1, n_expert):
+            ret_copy(src, expert_peer(p), me_e).start()
+        retrecv[src, chunk(me_e), :] = retsend[src, chunk(me_e), :]
+
+    def return_own():
+        part_copy().wait_recv()
+        total = retsend[chip, :, :dim].astype(F32) + part[:, :dim].astype(F32)
+        retsend[chip, :, :dim] = total.astype(BF16)
+        pair = join_pair(retsend[chip, :, dim:]) + join_pair(part[:, dim:])
+        retsend[chip, :, dim:] = split_pair(pair, width)
+        send_return(chip)
+
     def stage_return(src):
         for lane in range(CORES):
             g = src * CORES + lane
@@ -257,9 +274,14 @@
         retsend[src, :, :dim] = total.astype(BF16)
         pair = join_pair(dx[g, :, dim:]) + join_pair(dxrecv[src, :, dim:]) + bias
         retsend[src, :, dim:] = split_pair(pair, width)
-        for p in range(1, n_expert):
-            ret_copy(src, expert_peer(p), me_e).start()
-        retrecv[src, chunk(me_e), :] = retsend[src, chunk(me_e), :]
+
+        @pl.when(src == partner)
+        def _():
+            part_copy().start()
+
+        @pl.when((src != partner) & (src != chip))
+        def _():
+            send_return(src)
 
     def in_halves(one, two):
         lane = lax.broadcasted_iota(jnp.int32, (toks, LANES), 1)
@@ -344,10 +366,17 @@
         @pl.when(step >= 1)
         def _():
             stage_rows(order(step - 1))
+
+        @pl.when(step == chips)
+        def _():
+            return_own()
+
+        @pl.when(step >= 1)
+        def _():
             stage_compute(order(step - 1))
             stage_return(order(step - 1))
 
-        @pl.when(step >= 2)
+        @pl.when(step == chips)
         def _():
             stage_combine(order(step - 2))
 
@@ -362,6 +391,7 @@
 
     weights_in(0, dim // 2)
     stage_combine(order(chips - 1))
+    stage_combine(chip)
     weights_in(dim // 2, dim)
     store_in = pltpu.make_async_copy(gwi_ref, gwi_hbm, loc.at[5])
     store_in.start()
@@ -379,8 +409,8 @@
     ext = facc[:, dim:]
     one, two = ext[:, 0:1], ext[:, LANES // 2 : LANES // 2 + 1]
     lane = lax.broadcasted_iota(jnp.int32, (toks, LANES), 1)
-    for p in range(1, chips):
-        other = chip_peer(p)
+    for p in range(chips // 2):
+        other = base + p
         fin_copy(other, other).wait_recv()
         total = total + frecv[other, :, :dim].astype(F32)
         ext = frecv[other, :, dim:].astype(F32)
@@ -397,9 +427,9 @@
     store_in.wait()
     store_out.wait()
 
-    for p in range(1, chips):
-        other = chip_peer(p)
-        fin_copy(other, chip).wait_send()
+    part_copy().wait_send()
+    for p in range(chips // 2):
+        fin_copy(base + p, chip).wait_send()
     for src in range(chips):
         @pl.when((src <= chip) & (chip < chips - 1))
         def _():
@@ -411,23 +441,34 @@
 
         for p in range(1, n_expert):
             xy_copy(src, expert_peer(p), me_e).wait_send()
-            ret_copy(src, expert_peer(p), me_e).wait_send()
+
+        @pl.when(src != partner)
+        def _():
+            for p in range(1, n_expert):
+                ret_copy(src, expert_peer(p), me_e).wait_send()
+
         for e in range(n_expert):
             sib_copy(src, e, core).wait_send()
         dx_copy(src, 1 - core).wait_send()
 
 
-def hand_over(a_in, b_in, c_in, a_out, b_out, c_out, sems):
-    copies = []
-    for i, (src, dst) in enumerate(((a_in, a_out), (b_in, b_out), (c_in, c_out))):
-        part = src.shape[0] // 4
-        for j in range(4):
-            at = pl.ds(j * part, part)
-            copies.append(pltpu.make_async_copy(src.at[at], dst.at[at], sems.at[4 * i + j]))
-    for copy in copies:
-        copy.start()
-    for copy in copies:
-        copy.wait()
+def hand_over(a_in, b_in, c_in, a_out, b_out, c_out, a_mid, b_mid, c_mid, sems):
+    loads, stores = [], []
+    for i, (src, mid, dst) in enumerate(
+        ((b_in, b_mid, b_out), (c_in, c_mid, c_out), (a_in, a_mid, a_out))
+    ):
+        part = src.shape[0] // 2
+        for j in range(2):
+            at, k = pl.ds(j * part, part), 2 * i + j
+            loads.append(pltpu.make_async_copy(src.at[at], mid.at[at], sems.at[0, k]))
+            stores.append(pltpu.make_async_copy(mid.at[at], dst.at[at], sems.at[1, k]))
+    for load in loads:
+        load.start()
+    for load, store in zip(loads, stores):
+        load.wait()
+        store.start()
+    for store in stores:
+        store.wait()
 
 
 def scratch_sizes(n_expert, chips, cap, toks, dim, units):
@@ -462,7 +503,7 @@
     chips = n_zero // CORES
     sizes = scratch_sizes(n_expert, chips, cap, toks, dim, units)
     held = sum(functools.reduce(lambda a, b: a * b, s) * jnp.dtype(t).itemsize for s, t in sizes)
-    if held > (46 << 20) or n_expert * cap > 256 or n_zero % CORES or chips < 3:
+    if held > (46 << 20) or n_expert * cap > 256 or n_zero % CORES or chips != 4:
         return plain_device(
             tokens, grads_out, routes, slots, combine, w_in, b_in, w_out, b_out
         )
@@ -492,6 +533,8 @@
             sem((chips, n_expert)), sem((chips, n_expert)),
             sem((chips,)), sem((chips,)),
             sem((7,)),
+            pltpu.VMEM((n_expert * cap, dim + LANES), BF16),
+            sem((2,)),
         ],
         compiler_params=pltpu.CompilerParams(
             collective_id=0, has_side_effects=True, vmem_limit_bytes=60 << 20
@@ -504,7 +547,7 @@
         out_shape=tuple(jax.ShapeDtypeStruct(a.shape, a.dtype) for a in (gt, gwi, gwo)),
         in_specs=[hbm] * 3,
         out_specs=(hbm,) * 3,
-        scratch_shapes=[sem((12,))],
+        scratch_shapes=[pltpu.VMEM(a.shape, a.dtype) for a in (gt, gwi, gwo)] + [sem((2, 6))],
         compiler_params=pltpu.CompilerParams(vmem_limit_bytes=60 << 20),
         name="hand_over",
     )(gt, gwi, gwo)

time: 185 us -> 103 us (0.56)
  Pallas kernels: 180 us -> 97.8 us
    pallas_call x1, Pallas kernels: 72.7 us -> 2.57 us  [on_device(): pl.pallas_call(hand_over, out_shape=tuple((jax.ShapeDtypeStruct(a.shape,...]
    pallas_call x1, Pallas kernels: 107 us -> 95.2 us  [on_device(): pl.pallas_call(functools.partial(fused_kernel, n_expert, chips, cap), out...]
where the time goes in v5:
time: 103 us
  Pallas kernels  97.8 us (95%)
  local copies, waits for them, and re-layouts  3.99 us (4%)
    pallas_call x1, Pallas kernels, on_device(): pl.pallas_call(functools.partial(fused_kernel, n_expert, chips, cap), out...  95.2 us
    unnamed x15, local copies, waits for them, and re-layouts  3.26 us
    pallas_call x1, Pallas kernels, on_device(): pl.pallas_call(hand_over, out_shape=tuple((jax.ShapeDtypeStruct(a.shape,...  2.57 us

profile of v5, /device:TPU:0, one launch (start us, length us, event | category | flops | bytes accessed | tf_op | source)
XLA Modules:
  0.0 102.5 jit_solution(4440798161755442697)
XLA Ops:
  0.6 0.0 copy-start.4
  0.6 0.0 copy-start.3
  0.7 0.7 copy-done.4
  1.3 0.0 copy-done.3
  1.3 0.0 copy-start.5
  1.3 0.6 copy-done.5
  2.0 0.7 copy.17.meta_hbm
  2.7 95.2 %routed_expert_backward.1 = (bf16[128,1024]{1,0:T(8,128)(2,1)}, f32[128,2]{1,0:T(8,128)}, bf16[1024,512]{1,0:T(8,128)(2,1)}, f32[1,512]{1,0:T(1,128)}, bf16[512,1024]{1,0:T(8,128)(2,1)}, /*index=5*/f32[1,1024]{1,0:T(1,128)}) custom-call(bf16[128,1024]{1,0:T(8,128)(2,1)} %x_hbm.1, bf16[128,1024]{1,0:T(8,128)(2,1)} %g_hbm.1, bf16[128,128]{1,0:T(8,128)(2,1)} %copy.17.meta_hbm, ...), custom_call_target="tpu_custom_call" | custom-call | tf_op jit(solution)/shard_map/routed_expert_backward/pallas_call | solution.py:515
  98.0 0.0 copy-start
  98.0 2.6 %hand_over.1 = (bf16[128,1024]{1,0:T(8,128)(2,1)}, bf16[1024,512]{1,0:T(8,128)(2,1)}, bf16[512,1024]{1,0:T(8,128)(2,1)}) custom-call(bf16[128,1024]{1,0:T(8,128)(2,1)} %get-tuple-element.15.a_in, bf16[1024,512]{1,0:T(8,128)(2,1)} %get-tuple-element.16.b_in, bf16[512,1024]{1,0:T(8,128)(2,1)} %get-tuple-element.17.c_in), custom_call_target="tpu_custom_call" | custom-call | tf_op jit(solution)/shard_map/hand_over/pallas_call | solution.py:545
  100.6 0.0 copy-done
  100.6 0.0 copy-start.2
  100.6 0.6 copy.18
  101.2 0.0 copy-done.2
  101.3 0.0 copy-start.1
  101.3 0.6 copy.21
  101.8 0.1 copy-done.1
  101.9 0.6 copy.22
  (3 shorter events, 0.0 us)
Async XLA Ops:
  0.6 0.7 copy-start.4
  0.6 0.7 copy-start.3
  1.3 0.7 copy-start.5
  98.0 2.6 %copy-start = (f32[128,2]{1,0:T(8,128)S(1)}, f32[128,2]{1,0:T(8,128)}, u32[]{:S(2)}) copy-start(f32[128,2]{1,0:T(8,128)} %get-tuple-element.31) | copy-start | bytes 3076
  100.6 0.7 copy-start.2
  101.3 0.7 copy-start.1

commit v6 on v5

--- a/solution.py
+++ b/solution.py
@@ -94,10 +94,11 @@
 
 
 def fused_kernel(
-    n_expert, chips, cap, x_hbm, g_hbm, meta_hbm, w_in_hbm, b_in_ref, w_out_hbm, b_out_ref,
+    n_expert, chips, cap, x_hbm, g_hbm, routes_ref, slots_ref, combine_ref, w_in_hbm, b_in_ref, w_out_hbm, b_out_ref,
     gt_ref, gc_ref, gwi_hbm, gbi_ref, gwo_hbm, gbo_ref,
     w_in_ref, w_out_ref, gwi_ref, gwo_ref, tok, sendbuf, rows, hid, dpre, dout, dx, dxrecv, retsend, retrecv, fsend, frecv, facc,
     tok_s, tok_r, xy_s, xy_r, sib_s, sib_r, dx_s, dx_r, ret_s, ret_r, fin_s, fin_r, loc, part, part_sem,
+    mtok, mtok_s, mtok_r,
 ):
     me_e = lax.axis_index("expert")
     me_z = lax.axis_index("zero")
@@ -137,22 +138,35 @@
             (me_e, to * CORES + core),
         )
 
+    def meta_copy(src, way):
+        to = chip + (1 if way else -1)
+        return remote(
+            mtok.at[src], mtok.at[src], mtok_s.at[way, src], mtok_r.at[src],
+            (me_e, to * CORES + core),
+        )
+
+    def send_tokens(src, way):
+        meta_copy(src, way).start()
+        tok_copy(src, way).start()
+
     def pass_tokens(away):
         @pl.when(chip >= away)
         def _():
+            meta_copy(chip - away, 1).wait_recv()
             tok_copy(chip - away, 1).wait_recv()
 
             @pl.when(chip < chips - 1)
             def _():
-                tok_copy(chip - away, 1).start()
+                send_tokens(chip - away, 1)
 
         @pl.when(chip + away < chips)
         def _():
+            meta_copy(chip + away, 0).wait_recv()
             tok_copy(chip + away, 0).wait_recv()
 
             @pl.when(chip > 0)
             def _():
-                tok_copy(chip + away, 0).start()
+                send_tokens(chip + away, 0)
 
     def xy_copy(src, peer, frm):
         return remote(
@@ -188,28 +202,32 @@
             fsend.at[to], frecv.at[frm], fin_s.at[to], fin_r.at[frm], (me_e, to * CORES + core)
         )
 
+    def fill_meta():
+        slot = slots_ref[...]
+        place = jnp.where(slot < cap, routes_ref[...] * cap + slot, -1).astype(F32)
+        share = combine_ref[...].astype(F32)
+        row = lax.broadcasted_iota(jnp.int32, mtok.shape[1:], 0)
+        value = jnp.zeros(mtok.shape[1:], F32)
+        for i, line in enumerate((place[0:1], place[1:2], share[0:1], share[1:2])):
+            value = jnp.where(row == i, line, value)
+        mtok[chip] = value.astype(BF16)
+
     def picks_of(src):
-        meta = tok[src, :, 2 * dim :].astype(F32)
-        spots = lax.broadcasted_iota(jnp.int32, (toks, width), 1).astype(F32)
-        quarter = LANES // 4
-        first = jnp.where(meta[:, 0:1] == spots, 1.0, 0.0)
-        second = jnp.where(meta[:, quarter : quarter + 1] == spots, 1.0, 0.0)
+        meta = mtok[src].astype(F32)
+        spots = lax.broadcasted_iota(jnp.int32, (width, toks), 0).astype(F32)
+        first = jnp.where(meta[0:1] == spots, 1.0, 0.0)
+        second = jnp.where(meta[1:2] == spots, 1.0, 0.0)
         return first, second, meta
 
     def stage_tokens(src):
         first, second, meta = picks_of(src)
-        quarter = LANES // 4
-        both = (first + second).T.astype(BF16)
+        both = (first + second).astype(BF16)
         step = 512
         for col in range(0, 2 * dim, step):
             out = matmul(both, tok[src, :, col : col + step], ((1,), (0,)))
             sendbuf[src, :, col : col + step] = out.astype(BF16)
-        w0 = jnp.broadcast_to(meta[:, 2 * quarter : 2 * quarter + 1], (toks, LANES)).astype(BF16)
-        w1 = jnp.broadcast_to(meta[:, 3 * quarter : 3 * quarter + 1], (toks, LANES)).astype(BF16)
-        out = matmul(first.T.astype(BF16), w0, ((1,), (0,))) + matmul(
-            second.T.astype(BF16), w1, ((1,), (0,))
-        )
-        sendbuf[src, :, 2 * dim :] = out.astype(BF16)
+        share = jnp.sum(first * meta[2:3] + second * meta[3:4], axis=1, keepdims=True)
+        sendbuf[src, :, 2 * dim :] = jnp.broadcast_to(share, (width, LANES)).astype(BF16)
         for p in range(1, n_expert):
             xy_copy(src, expert_peer(p), me_e).start()
         rows[src * CORES + core, chunk(me_e), :] = sendbuf[src, chunk(me_e), :]
@@ -293,10 +311,10 @@
             ret_copy(src, peer, peer).wait_recv()
         first, second, _ = picks_of(src)
         both = (first + second).astype(BF16)
-        grads = matmul(both, retrecv[src, :, :dim], ((1,), (0,)))
+        grads = matmul(both, retrecv[src, :, :dim], ((0,), (0,)))
         ext = retrecv[src, :, dim:]
-        one = join_pair(matmul(first.astype(BF16), ext, ((1,), (0,))))
-        two = join_pair(matmul(second.astype(BF16), ext, ((1,), (0,))))
+        one = join_pair(matmul(first.astype(BF16), ext, ((0,), (0,))))
+        two = join_pair(matmul(second.astype(BF16), ext, ((0,), (0,))))
 
         @pl.when(src == chip)
         def _():
@@ -329,24 +347,24 @@
         for i, (src, dst) in enumerate((
             (x_hbm, tok.at[chip, :, :dim]),
             (g_hbm, tok.at[chip, :, dim : 2 * dim]),
-            (meta_hbm, tok.at[chip, :, 2 * dim :]),
             (w_in_hbm, w_in_ref),
             (w_out_hbm, w_out_ref),
         ))
     ]
     for load in loads:
         load.start()
-    for load in loads[:3]:
+    fill_meta()
+    for load in loads[:2]:
         load.wait()
     pl.semaphore_wait(barrier, n_expert + chips - 1)
 
     @pl.when(chip < chips - 1)
     def _():
-        tok_copy(chip, 1).start()
+        send_tokens(chip, 1)
 
     @pl.when(chip > 0)
     def _():
-        tok_copy(chip, 0).start()
+        send_tokens(chip, 0)
 
     @pl.loop(0, chips + 1)
     def _(step):
@@ -360,7 +378,7 @@
 
         @pl.when(step == 0)
         def _():
-            for load in loads[3:]:
+            for load in loads[2:]:
                 load.wait()
 
         @pl.when(step >= 1)
@@ -422,8 +440,7 @@
             jnp.where(lane < LANES // 2, 0.0, ext), axis=1, keepdims=True
         )
     gt_ref[...] = total.astype(BF16)
-    gc_ref[:, 0:1] = one
-    gc_ref[:, 1:2] = two
+    gc_ref[...] = jnp.where(lane == 0, one, two).T[0:TOP]
     store_in.wait()
     store_out.wait()
 
@@ -433,10 +450,12 @@
     for src in range(chips):
         @pl.when((src <= chip) & (chip < chips - 1))
         def _():
+            meta_copy(src, 1).wait_send()
             tok_copy(src, 1).wait_send()
 
         @pl.when((src >= chip) & (chip > 0))
         def _():
+            meta_copy(src, 0).wait_send()
             tok_copy(src, 0).wait_send()
 
         for p in range(1, n_expert):
@@ -452,14 +471,15 @@
         dx_copy(src, 1 - core).wait_send()
 
 
-def hand_over(a_in, b_in, c_in, a_out, b_out, c_out, a_mid, b_mid, c_mid, sems):
+def hand_over(*refs):
+    count = (len(refs) - 1) // 3
+    sources, results, middles, sems = refs[:count], refs[count : 2 * count], refs[2 * count : -1], refs[-1]
     loads, stores = [], []
-    for i, (src, mid, dst) in enumerate(
-        ((b_in, b_mid, b_out), (c_in, c_mid, c_out), (a_in, a_mid, a_out))
-    ):
-        part = src.shape[0] // 2
-        for j in range(2):
-            at, k = pl.ds(j * part, part), 2 * i + j
+    for src, dst, mid in zip(sources, results, middles):
+        pieces = 2 if src.shape[0] >= 64 else 1
+        part = src.shape[0] // pieces
+        for j in range(pieces):
+            at, k = pl.ds(j * part, part), len(loads)
             loads.append(pltpu.make_async_copy(src.at[at], mid.at[at], sems.at[0, k]))
             stores.append(pltpu.make_async_copy(mid.at[at], dst.at[at], sems.at[1, k]))
     for load in loads:
@@ -478,7 +498,7 @@
         ((units, dim), BF16),
         ((dim, units), BF16),
         ((units, dim), BF16),
-        ((chips, toks, 2 * dim + LANES), BF16),
+        ((chips, toks, 2 * dim), BF16),
         ((chips, width, 2 * dim + LANES), BF16),
         ((groups, width, 2 * dim + LANES), BF16),
         ((groups, width, units), BF16),
@@ -503,12 +523,10 @@
     chips = n_zero // CORES
     sizes = scratch_sizes(n_expert, chips, cap, toks, dim, units)
     held = sum(functools.reduce(lambda a, b: a * b, s) * jnp.dtype(t).itemsize for s, t in sizes)
-    if held > (46 << 20) or n_expert * cap > 256 or n_zero % CORES or chips != 4:
+    if held > (46 << 20) or n_expert * cap > 256 or n_zero % CORES or chips != 4 or toks != LANES:
         return plain_device(
             tokens, grads_out, routes, slots, combine, w_in, b_in, w_out, b_out
         )
-    places = jnp.where(slots < cap, routes * cap + slots, -1).astype(BF16)
-    meta = jnp.repeat(jnp.concatenate([places, combine], axis=1), LANES // 4, axis=1)
     vmem = pl.BlockSpec(memory_space=pltpu.VMEM)
     hbm = pl.BlockSpec(memory_space=pl.ANY)
     sem = pltpu.SemaphoreType.DMA
@@ -516,13 +534,13 @@
         functools.partial(fused_kernel, n_expert, chips, cap),
         out_shape=(
             jax.ShapeDtypeStruct((toks, dim), BF16),
-            jax.ShapeDtypeStruct((toks, TOP), F32),
+            jax.ShapeDtypeStruct((TOP, toks), F32),
             jax.ShapeDtypeStruct((dim, units), BF16),
             jax.ShapeDtypeStruct((1, units), F32),
             jax.ShapeDtypeStruct((units, dim), BF16),
             jax.ShapeDtypeStruct((1, dim), F32),
         ),
-        in_specs=[hbm, hbm, hbm, hbm, vmem, hbm, vmem],
+        in_specs=[hbm, hbm, vmem, vmem, vmem, hbm, vmem, hbm, vmem],
         out_specs=(vmem, vmem, hbm, vmem, hbm, vmem),
         scratch_shapes=[pltpu.VMEM(s, t) for s, t in sizes]
         + [
@@ -535,23 +553,26 @@
             sem((7,)),
             pltpu.VMEM((n_expert * cap, dim + LANES), BF16),
             sem((2,)),
+            pltpu.VMEM((chips, 16, toks), BF16),
+            sem((2, chips)),
+            sem((chips,)),
         ],
         compiler_params=pltpu.CompilerParams(
             collective_id=0, has_side_effects=True, vmem_limit_bytes=60 << 20
         ),
         name="routed_expert_backward",
-    )(tokens, grads_out, meta, w_in[0], b_in, w_out[0], b_out)
-    gt, gc, gwi, gbi, gwo, gbo = outs
-    gt, gwi, gwo = pl.pallas_call(
+    )(tokens, grads_out, routes.T, slots.T, combine.T, w_in[0], b_in, w_out[0], b_out)
+    outs = pl.pallas_call(
         hand_over,
-        out_shape=tuple(jax.ShapeDtypeStruct(a.shape, a.dtype) for a in (gt, gwi, gwo)),
-        in_specs=[hbm] * 3,
-        out_specs=(hbm,) * 3,
-        scratch_shapes=[pltpu.VMEM(a.shape, a.dtype) for a in (gt, gwi, gwo)] + [sem((2, 6))],
+        out_shape=tuple(jax.ShapeDtypeStruct(a.shape, a.dtype) for a in outs),
+        in_specs=[hbm] * len(outs),
+        out_specs=(hbm,) * len(outs),
+        scratch_shapes=[pltpu.VMEM(a.shape, a.dtype) for a in outs] + [sem((2, 12))],
         compiler_params=pltpu.CompilerParams(vmem_limit_bytes=60 << 20),
         name="hand_over",
-    )(gt, gwi, gwo)
-    return (gt, gc, gwi[None], gbi, gwo[None], gbo)
+    )(*outs)
+    gt, gc, gwi, gbi, gwo, gbo = outs
+    return (gt, gc.T, gwi[None], gbi, gwo[None], gbo)
 
 
 def solution(mesh):

time: 103 us -> 97.7 us (0.949)
  local copies, waits for them, and re-layouts: 3.99 us -> 0 us
    unnamed x15 -> x0, local copies, waits for them, and re-layouts: 3.26 us -> none
    pallas_call x1, Pallas kernels: 95.2 us -> 94.1 us  [on_device(): pl.pallas_call(functools.partial(fused_kernel, n_expert, chips, cap), out...]
where the time goes in v6:
time: 97.7 us; the launch traced here: 97.5 us
  Pallas kernels  96.8 us (99%)
    pallas_call x1, Pallas kernels, on_device(): pl.pallas_call(functools.partial(fused_kernel, n_expert, chips, cap), out...  94.1 us
    pallas_call x1, Pallas kernels, on_device(): pl.pallas_call(hand_over, out_shape=tuple((jax.ShapeDtypeStruct(a.shape,...  2.71 us

profile of v6, /device:TPU:0, one launch (start us, length us, event | category | flops | bytes accessed | tf_op | source)
XLA Modules:
  0.0 97.5 jit_solution(13964091447741195637)
XLA Ops:
  0.6 94.1 %routed_expert_backward.1 = (bf16[128,1024]{1,0:T(8,128)(2,1)}, f32[2,128]{1,0:T(2,128)}, bf16[1024,512]{1,0:T(8,128)(2,1)}, f32[1,512]{1,0:T(1,128)}, bf16[512,1024]{1,0:T(8,128)(2,1)}, /*index=5*/f32[1,1024]{1,0:T(1,128)}) custom-call(bf16[128,1024]{1,0:T(8,128)(2,1)} %x_hbm.1, bf16[128,1024]{1,0:T(8,128)(2,1)} %g_hbm.1, s32[2,128]{1,0:T(2,128)} %bitcast.10, ...), custom_call_target="tpu_custom_call" | custom-call | tf_op jit(solution)/shard_map/routed_expert_backward/pallas_call | solution.py:533
  94.8 2.7 %hand_over.1 = (bf16[128,1024]{1,0:T(8,128)(2,1)}, f32[2,128]{1,0:T(2,128)}, bf16[1024,512]{1,0:T(8,128)(2,1)}, f32[1,512]{1,0:T(1,128)}, bf16[512,1024]{1,0:T(8,128)(2,1)}, /*index=5*/f32[1,1024]{1,0:T(1,128)}) custom-call(bf16[128,1024]{1,0:T(8,128)(2,1)} %get-tuple-element.18.refs_0_, f32[2,128]{1,0:T(2,128)} %get-tuple-element.19.refs_1_, ...), custom_call_target="tpu_custom_call" | custom-call | tf_op jit(solution)/shard_map/hand_over/pallas_call | solution.py:565

commit v7 on v6

--- a/solution.py
+++ b/solution.py
@@ -270,13 +270,14 @@
             ret_copy(src, expert_peer(p), me_e).start()
         retrecv[src, chunk(me_e), :] = retsend[src, chunk(me_e), :]
 
-    def return_own():
+    def add_part():
+        grads = rows[chip * CORES + core, :, dim : 2 * dim].astype(F32)
+        bias = jnp.sum(grads * b_out_ref[...].astype(F32), axis=1, keepdims=True)
         part_copy().wait_recv()
         total = retsend[chip, :, :dim].astype(F32) + part[:, :dim].astype(F32)
         retsend[chip, :, :dim] = total.astype(BF16)
-        pair = join_pair(retsend[chip, :, dim:]) + join_pair(part[:, dim:])
+        pair = join_pair(retsend[chip, :, dim:]) + join_pair(part[:, dim:]) + bias
         retsend[chip, :, dim:] = split_pair(pair, width)
-        send_return(chip)
 
     def stage_return(src):
         for lane in range(CORES):
@@ -284,13 +285,10 @@
             weight = rows[g, :, 2 * dim :].astype(F32)[:, 0:1]
             dout[g] = (weight * rows[g, :, dim : 2 * dim].astype(F32)).astype(BF16)
         g = src * CORES + core
-        grads = rows[g, :, dim : 2 * dim].astype(F32)
-        bias = jnp.sum(grads * b_out_ref[...].astype(F32), axis=1, keepdims=True)
-        bias = bias * jnp.where(src == chip, 1.0, 0.0)
         dx_copy(src, core).wait_recv()
         total = dx[g, :, :dim].astype(F32) + dxrecv[src, :, :dim].astype(F32)
         retsend[src, :, :dim] = total.astype(BF16)
-        pair = join_pair(dx[g, :, dim:]) + join_pair(dxrecv[src, :, dim:]) + bias
+        pair = join_pair(dx[g, :, dim:]) + join_pair(dxrecv[src, :, dim:])
         retsend[src, :, dim:] = split_pair(pair, width)
 
         @pl.when(src == partner)
@@ -381,13 +379,17 @@
             for load in loads[2:]:
                 load.wait()
 
+        @pl.when(step == chips)
+        def _():
+            add_part()
+
         @pl.when(step >= 1)
         def _():
             stage_rows(order(step - 1))
 
         @pl.when(step == chips)
         def _():
-            return_own()
+            send_return(chip)
 
         @pl.when(step >= 1)
         def _():

time: 97.7 us -> 97.3 us (level)
  no operation moved by 1% of the time
where the time goes in v7:
time: 97.3 us; the launch traced here: 97.1 us
  Pallas kernels  96.5 us (99%)
    pallas_call x1, Pallas kernels, on_device(): pl.pallas_call(functools.partial(fused_kernel, n_expert, chips, cap), out...  93.8 us
    pallas_call x1, Pallas kernels, on_device(): pl.pallas_call(hand_over, out_shape=tuple((jax.ShapeDtypeStruct(a.shape,...  2.71 us

profile of v7, /device:TPU:0, one launch (start us, length us, event | category | flops | bytes accessed | tf_op | source)
XLA Modules:
  0.0 97.1 jit_solution(14353395479353154327)
XLA Ops:
  0.6 93.8 %routed_expert_backward.1 = (bf16[128,1024]{1,0:T(8,128)(2,1)}, f32[2,128]{1,0:T(2,128)}, bf16[1024,512]{1,0:T(8,128)(2,1)}, f32[1,512]{1,0:T(1,128)}, bf16[512,1024]{1,0:T(8,128)(2,1)}, /*index=5*/f32[1,1024]{1,0:T(1,128)}) custom-call(bf16[128,1024]{1,0:T(8,128)(2,1)} %x_hbm.1, bf16[128,1024]{1,0:T(8,128)(2,1)} %g_hbm.1, s32[2,128]{1,0:T(2,128)} %bitcast.10, ...), custom_call_target="tpu_custom_call" | custom-call | tf_op jit(solution)/shard_map/routed_expert_backward/pallas_call | solution.py:535
  94.4 2.7 %hand_over.1 = (bf16[128,1024]{1,0:T(8,128)(2,1)}, f32[2,128]{1,0:T(2,128)}, bf16[1024,512]{1,0:T(8,128)(2,1)}, f32[1,512]{1,0:T(1,128)}, bf16[512,1024]{1,0:T(8,128)(2,1)}, /*index=5*/f32[1,1024]{1,0:T(1,128)}) custom-call(bf16[128,1024]{1,0:T(8,128)(2,1)} %get-tuple-element.18.refs_0_, f32[2,128]{1,0:T(2,128)} %get-tuple-element.19.refs_1_, ...), custom_call_target="tpu_custom_call" | custom-call | tf_op jit(solution)/shard_map/hand_over/pallas_call | solution.py:567
